TPU v7x, 256 devices: a whole 4x4x8 slice. The times are simulated.
256 devices in a mesh: mode: 16 (over x, y_lo, core), wall: 16 (over y_hi, z).
Axes of the slice: x: 4, y: 4 (y_hi: 2, y_lo: 2; y = y_hi * 2 + y_lo), z: 8, core: 2. Of those that a mesh axis runs over, the one named last changes fastest.
Arguments:
- vectors: bfloat16 [2, 2560, 8192], P(None, 'wall', 'mode'), may hold values from -6 to 6
- coupling: bfloat16 [5, 2, 2560, 2560], P(None, None, 'wall'), may hold values from -0.0390625 to 0.0390625
- pattern: int32 [5, 16, 16], replicated, may hold values 0 or 1
Outputs:
- image: bfloat16 [2, 2560, 8192], P(None, 'wall', 'mode')
All inputs are finite; a program needn't handle non-finite values.
Results may differ from a plain program's by a relative error of at most 0.001.
Values may be sent and summed in bfloat16 or wider, within the bound.
No kernel may reach another device: no remote copies, remote signals or barrier semaphores. Data moves between devices by JAX's collectives and lax.ppermute only.
A program may use at most 128 MiB of HBM per device.

v0:
```python
import jax
import jax.numpy as jnp
from jax import lax
from jax.sharding import PartitionSpec as P

F = 5
BLK = 32
HARM = 64
HMAX = 2
MD = 32


def passed_along(value, axis, by):
    devices = lax.axis_size(axis)
    return lax.ppermute(value, axis, [(i, (i + by) % devices) for i in range(devices)])


def product(block, coup_re, coup_im):
    out_re = jnp.dot(coup_re, block[0], preferred_element_type=jnp.float32) - jnp.dot(
        coup_im, block[1], preferred_element_type=jnp.float32
    )
    out_im = jnp.dot(coup_im, block[0], preferred_element_type=jnp.float32) + jnp.dot(
        coup_re, block[1], preferred_element_type=jnp.float32
    )
    return jnp.stack([out_re, out_im])


def move_inputs(block, steps):
    return passed_along(block, "mode", steps)


def per_device(vectors, coupling, pattern):
    local_width = coupling.shape[2]
    harmonics = coupling.shape[0]
    shards = lax.axis_size("mode")
    local_cols = vectors.shape[2]
    modes_dev = MD
    local_blocks = local_width // (F * BLK)
    first_block = lax.axis_index("wall") * local_blocks
    local_pattern = lax.dynamic_slice_in_dim(pattern, first_block, local_blocks, 2)
    turned = jnp.transpose(local_pattern, (0, 2, 1))
    grown = jnp.repeat(jnp.repeat(turned, BLK * F, axis=1), BLK * F, axis=2)
    masked = coupling * grown[:, None].astype(jnp.bfloat16)
    distances = [(harmonic - HMAX) * HARM // modes_dev % shards for harmonic in range(harmonics)]
    zeros = jnp.zeros((2, local_width, local_cols), jnp.float32)
    gathered = lax.all_gather(vectors, "wall", axis=1, tiled=True)
    total = zeros
    for harmonic in range(harmonics):
        steps = distances[harmonic]
        moved = gathered if steps == 0 else move_inputs(gathered, steps)
        total = total + product(moved, masked[harmonic, 0], masked[harmonic, 1])
    return total.astype(jnp.bfloat16)


def solution(mesh):
    placed = (P(None, "wall", "mode"), P(None, None, "wall", None), P())
    return jax.shard_map(
        per_device, mesh=mesh, in_specs=placed, out_specs=P(None, "wall", "mode"), check_vma=False
    )
```

profile of v0, /device:TPU:16, one launch (start us, length us, event | category | flops | bytes accessed | tf_op | source)
XLA Modules:
  0.0 387.5 jit_solution(7530511646448792827)
XLA Ops:
  6.5 0.7 all-gather.2.cloned.1.call-update
  7.3 110.6 %all-gather.2.cloned.1.call-done = bf16[2,2560,512]{2,1,0:T(8,128)(2,1)} async-done(((bf16[2,160,512]{2,1,0:T(8,128)(2,1)}), bf16[2,2560,512]{2,1,0:T(8,128)(2,1)}) %all-gather.2.cloned.1.call-update) | async-done | bytes 5242896 | tf_op jit(solution)/shard_map/all_gather | solution.py:46
  117.8 2.1 collective-permute-start.2
  119.9 1.5 collective-permute-start.3
  121.4 2.0 collective-permute-start.1
  123.5 0.6 collective-permute-start
  124.2 0.1 copy.5
  124.3 0.1 broadcast_in_dim.4
  124.4 0.1 convert_element_type.18
  124.5 7.0 %broadcast_multiply_fusion = bf16[5,2,160,2560]{3,2,1,0:T(8,128)(2,1)} fusion(bf16[5,2,160,2560]{3,2,1,0:T(8,128)(2,1)} %param.4, bf16[5,2560]{1,0:T(8,128)(2,1)S(1)} %convert_element_type.18), kind=kLoop, calls=%fused_computation | loop fusion | flops 4096000 | bytes 16409600 | tf_op jit(solution)/shard_map/mul | solution.py:43
  131.5 2.7 fusion.8
  134.3 3.2 fusion.9
  137.5 2.3 fusion.34
  139.9 0.6 fusion.35
  140.5 201.8 %collective-permute-done.2 = bf16[2,2560,512]{2,1,0:T(8,128)(2,1)} collective-permute-done((bf16[2,2560,512]{2,1,0:T(8,128)(2,1)}, bf16[2,2560,512]{2,1,0:T(8,128)(2,1)}, u32[]{:S(2)}, u32[]{:S(2)}) %collective-permute-start.2) | collective-permute-done | bytes 5242912 | tf_op jit(solution)/shard_map/ppermute | solution.py:15
  342.2 2.3 fusion.14
  344.5 2.3 fusion.15
  346.9 2.3 fusion.18
  349.2 2.3 fusion.19
  351.6 2.3 fusion.7
  353.9 2.3 fusion.6
  356.2 2.3 fusion.3
  358.6 2.3 fusion.2
  360.9 2.3 fusion.36
  363.3 2.3 fusion.37
  365.6 2.3 fusion.38
  367.9 2.3 fusion.39
  370.3 2.3 fusion.33
  372.6 2.3 fusion.32
  375.0 2.3 fusion.31
  377.3 2.3 fusion.30
  379.6 1.0 fusion.43
  (12 shorter events, 0.1 us)
Async XLA Ops:
  6.5 117.5 %copy-start = (s32[5,16,16]{2,1,0:T(8,128)S(1)}, s32[5,16,16]{2,1,0:T(8,128)}, u32[]{:S(2)}) copy-start(s32[5,16,16]{2,1,0:T(8,128)} %param.5) | copy-start | bytes 15364
  6.5 111.3 %all-gather.2.cloned.1.call-start = ((), (), s32[]{:S(2)}) async-start(), calls=%async_computation | async-start | bytes 5570560 | tf_op jit(solution)/shard_map/all_gather | solution.py:46
  117.8 224.4 %collective-permute-start.2 = (bf16[2,2560,512]{2,1,0:T(8,128)(2,1)}, bf16[2,2560,512]{2,1,0:T(8,128)(2,1)}, u32[]{:S(2)}, u32[]{:S(2)}) collective-permute-start(bf16[2,2560,512]{2,1,0:T(8,128)(2,1)} %all-gather.2.cloned.1.call-done), channel_id=1, source_target_pairs={{0,32},{16,48},{32,64},{48,80},{64,96},{80,112},{96,128},{112,144}... | collective-permute-start | bytes 15728648 | tf_op jit(solution)/shard_map/ppermute | solution.py:15
  119.9 227.0 %collective-permute-start.3 = (bf16[2,2560,512]{2,1,0:T(8,128)(2,1)}, bf16[2,2560,512]{2,1,0:T(8,128)(2,1)}, u32[]{:S(2)}, u32[]{:S(2)}) collective-permute-start(bf16[2,2560,512]{2,1,0:T(8,128)(2,1)} %all-gather.2.cloned.1.call-done), channel_id=1, source_target_pairs={{0,64},{16,80},{32,96},{48,112},{64,128},{80,144},{96,160},{112,17... | collective-permute-start | bytes 15728648 | tf_op jit(solution)/shard_map/ppermute | solution.py:15
  121.4 230.1 %collective-permute-start.1 = (bf16[2,2560,512]{2,1,0:T(8,128)(2,1)}, bf16[2,2560,512]{2,1,0:T(8,128)(2,1)}, u32[]{:S(2)}, u32[]{:S(2)}) collective-permute-start(bf16[2,2560,512]{2,1,0:T(8,128)(2,1)} %all-gather.2.cloned.1.call-done), channel_id=1, source_target_pairs={{0,224},{16,240},{32,0},{48,16},{64,32},{80,48},{96,64},{112,80},{... | collective-permute-start | bytes 15728648 | tf_op jit(solution)/shard_map/ppermute | solution.py:15
  123.5 232.8 %collective-permute-start = (bf16[2,2560,512]{2,1,0:T(8,128)(2,1)}, bf16[2,2560,512]{2,1,0:T(8,128)(2,1)}, u32[]{:S(2)}, u32[]{:S(2)}) collective-permute-start(bf16[2,2560,512]{2,1,0:T(8,128)(2,1)} %all-gather.2.cloned.1.call-done), channel_id=1, source_target_pairs={{0,192},{16,208},{32,224},{48,240},{64,0},{80,16},{96,32},{112,48}... | collective-permute-start | bytes 15728648 | tf_op jit(solution)/shard_map/ppermute | solution.py:15
  131.5 6.0 %copy-start.1 = (bf16[5,2,160,2560]{3,2,1,0:T(8,128)(2,1)S(1)}, bf16[5,2,160,2560]{3,2,1,0:T(8,128)(2,1)}, u32[]{:S(2)}) copy-start(bf16[5,2,160,2560]{3,2,1,0:T(8,128)(2,1)} %broadcast_multiply_fusion) | copy-start | bytes 24576004
  134.3 5.6 %copy-start.2 = (bf16[2,2560,512]{2,1,0:T(8,128)(2,1)S(1)}, bf16[2,2560,512]{2,1,0:T(8,128)(2,1)}, u32[]{:S(2)}) copy-start(bf16[2,2560,512]{2,1,0:T(8,128)(2,1)} %all-gather.2.cloned.1.call-done) | copy-start | bytes 15728644
Sparse Core Ops, SparseCore 0:
  10.0 107.8 all-gather.1
where the time goes:
time: 390 us; the launch traced here: 388 us
  waiting for transfers between devices  313 us (80%)
  matrix products  46.1 us (12%)
  between operations  13.6 us (3%)
  other arithmetic  8.07 us (2%)
  starting transfers between devices  6.25 us (2%)
    ppermute x4, waiting for transfers between devices, passed_along(): lax.ppermute(value, axis, [(i, (i + by) % devices) for i in range(devices)])  202 us
    all_gather x1, waiting for transfers between devices, per_device(): gathered = lax.all_gather(vectors, 'wall', axis=1, tiled=True)  111 us
    dot_general x5, matrix products, product(): jnp.dot(coup_re, block[0], preferred_element_type=jnp.float32)  12.5 us
    dot_general x5, matrix products, product(): jnp.dot(coup_im, block[0], preferred_element_type=jnp.float32)  12 us
    dot_general x5, matrix products, product(): jnp.dot(coup_re, block[1], preferred_element_type=jnp.float32)  11.6 us
    dot_general x5, matrix products, product(): jnp.dot(coup_im, block[1], preferred_element_type=jnp.float32)  9.91 us
  transfers between devices with their start and end apart: 5, of which 2 were waited for; matrix products, arithmetic and copies ran while one was open for 8% of the time, Pallas kernels for 0%

commit v1 on v0

v1 whole, which is shorter than its diff:
```python
import functools

import jax
import jax.numpy as jnp
from jax import lax
from jax.experimental import pallas as pl
from jax.experimental.pallas import tpu as pltpu
from jax.sharding import PartitionSpec as P

F = 5
BLK = 32
ROWS = F * BLK
HMAX = 2
NOFF = 2 * HMAX + 1
Q = 8
HALF = 64
TILE = 2 * HALF
CORES = 2
WALL_Z = 8
WINDOW = 256
VMEM_BYTES = 48 * 2**20

MODE = ("mode", "wall")
GROUPS = [[2 * q + core for q in range(Q)] for core in range(CORES)]


def permutation(move):
    pairs = []
    for x in range(4):
        for y_lo in range(2):
            for core in range(CORES):
                for y_hi in range(2):
                    for z in range(WALL_Z):
                        nx, ny_lo, ny_hi, nz = move(x, y_lo, y_hi, z)
                        pairs.append((
                            ((x * 2 + y_lo) * CORES + core) * 16 + y_hi * WALL_Z + z,
                            ((nx * 2 + ny_lo) * CORES + core) * 16 + ny_hi * WALL_Z + nz,
                        ))
    return pairs


UP = permutation(lambda x, y_lo, y_hi, z: (x, y_lo, y_hi, (z + 1) % WALL_Z))
DOWN = permutation(lambda x, y_lo, y_hi, z: (x, y_lo, y_hi, (z - 1) % WALL_Z))
ACROSS = permutation(lambda x, y_lo, y_hi, z: (x, 1 - y_lo, 1 - y_hi, z))


def up(value):
    return lax.ppermute(value, MODE, UP)


def down(value):
    return lax.ppermute(value, MODE, DOWN)


def across(value):
    return lax.ppermute(value, MODE, ACROSS)


def pack_kernel(flip_ref, x_ref, out_ref):
    flip = flip_ref[0]
    for c in range(Q):
        cols = slice(c * HALF, (c + 1) * HALF)
        out_ref[c ^ flip] = jnp.concatenate([x_ref[0, :, cols], x_ref[1, :, cols]], axis=1)


def unpack_kernel(flip_ref, pieces_ref, out_ref):
    flip = flip_ref[0]
    for t in range(Q // 2):
        a = pieces_ref[(2 * t) ^ flip]
        b = pieces_ref[(2 * t + 1) ^ flip]
        cols = slice(t * TILE, (t + 1) * TILE)
        out_ref[0, :, cols] = jnp.concatenate([a[:, :HALF], b[:, :HALF]], axis=1)
        out_ref[1, :, cols] = jnp.concatenate([a[:, HALF:], b[:, HALF:]], axis=1)


def small_call(kernel, flip, value, shape):
    return pl.pallas_call(
        kernel,
        out_shape=jax.ShapeDtypeStruct(shape, value.dtype),
        in_specs=[pl.BlockSpec(memory_space=pltpu.SMEM), pl.BlockSpec(memory_space=pltpu.VMEM)],
        out_specs=pl.BlockSpec(memory_space=pltpu.VMEM),
        compiler_params=pltpu.CompilerParams(vmem_limit_bytes=VMEM_BYTES),
        cost_estimate=pl.CostEstimate(flops=0, bytes_accessed=4 * value.size, transcendentals=0),
    )(flip, value)


def product_kernel(blocks, first, last, walls_ref, here_ref, pattern_ref, *refs):
    x_refs = refs[:blocks]
    e_lo_ref, e_hi_ref = refs[blocks:blocks + 2]
    rest = refs[blocks + 2:]
    if first:
        acc_ref, padded_ref = rest
    elif last:
        acc_in_ref, out_ref, padded_ref, acc_ref = rest
    else:
        acc_in_ref, acc_ref, padded_ref = rest
    step = pl.program_id(0)
    here = here_ref[0]

    @pl.when(step == 0)
    def _():
        acc_ref[...] = jnp.zeros_like(acc_ref) if first else acc_in_ref[...]

    wall = walls_ref[step]
    offset = pl.multiple_of(lax.rem(wall, 4) * 32, 32)
    padded_ref[...] = jnp.zeros_like(padded_ref)
    for j in range(blocks):
        @pl.when(step == j)
        def _():
            padded_ref[1, :, pl.ds(offset, ROWS), :] = x_refs[j][...]

    left = jnp.concatenate(
        [
            jnp.concatenate(
                [jnp.concatenate([e_lo_ref[h, part], e_hi_ref[h, part]], axis=1) for h in range(NOFF)], axis=1
            )
            for part in range(2)
        ],
        axis=0,
    )
    present = [pattern_ref[(h * 16 + wall) * 16 + here] for h in range(NOFF)]
    for pair in range(Q // 2):
        q = 2 * pair
        right = jnp.concatenate(
            [
                jnp.concatenate(
                    [padded_ref[present[h], (q + k - (h - HMAX)) % Q] for k in range(2)], axis=1
                )
                for h in range(NOFF)
            ],
            axis=0,
        )
        result = jnp.dot(left, right, preferred_element_type=jnp.float32)
        acc_ref[q] += result[:, :TILE]
        acc_ref[q + 1] += result[:, TILE:]

    if last:
        @pl.when(step == blocks - 1)
        def _():
            lane = lax.broadcasted_iota(jnp.int32, (ROWS, TILE), 1)
            for q in range(Q):
                turned = pltpu.roll(acc_ref[q, ROWS:], HALF, 1)
                total = acc_ref[q, :ROWS] + jnp.where(lane < HALF, -turned, turned)
                out_ref[q] = total.astype(out_ref.dtype)


def product(xs, walls, here, pattern, coupling, acc, last):
    blocks = len(xs)
    first = acc is None
    whole = lambda shape: pl.BlockSpec(shape, lambda s, *_: (0,) * len(shape))
    acc_shape = (Q, 2 * ROWS, TILE)
    e_shape = (NOFF, 2, ROWS, 128)
    tile_at = lambda more: lambda s, walls, *_: (0, 0, 0, walls[s] * 5 // 4 + more)
    in_specs = [whole((Q, ROWS, TILE))] * blocks + [
        pl.BlockSpec(e_shape, tile_at(0)), pl.BlockSpec(e_shape, tile_at(1))
    ]
    operands = list(xs) + [coupling, coupling]
    scratch = [pltpu.VMEM((2, Q, WINDOW, TILE), jnp.bfloat16)]
    if not first:
        in_specs.append(whole(acc_shape))
        operands.append(acc)
    if last:
        scratch.append(pltpu.VMEM(acc_shape, jnp.float32))
        out_shape, out_spec = jax.ShapeDtypeStruct((Q, ROWS, TILE), jnp.bfloat16), whole((Q, ROWS, TILE))
    else:
        out_shape, out_spec = jax.ShapeDtypeStruct(acc_shape, jnp.float32), whole(acc_shape)
    flops = blocks * 2 * NOFF * WINDOW * 2 * ROWS * Q * TILE
    return pl.pallas_call(
        functools.partial(product_kernel, blocks, first, last),
        out_shape=out_shape,
        grid_spec=pltpu.PrefetchScalarGridSpec(
            num_scalar_prefetch=3, grid=(blocks,), in_specs=in_specs, out_specs=out_spec, scratch_shapes=scratch
        ),
        compiler_params=pltpu.CompilerParams(vmem_limit_bytes=VMEM_BYTES),
        cost_estimate=pl.CostEstimate(flops=flops, bytes_accessed=blocks * 1200000 + 2600000, transcendentals=0),
    )(walls, here, pattern, *operands)


def per_device(vectors, coupling, pattern):
    wall = lax.axis_index("wall")
    y_hi, z = wall // WALL_Z, lax.rem(wall, WALL_Z)
    flip = y_hi.reshape(1).astype(jnp.int32)
    here = wall.reshape(1).astype(jnp.int32)
    pattern = pattern.reshape(-1)

    pieces = small_call(pack_kernel, flip, vectors, (Q, ROWS, TILE))
    block = lax.all_to_all(pieces, "mode", 0, 0, axis_index_groups=GROUPS, tiled=True)

    own, other = {0: block}, {}

    def walls_of(names):
        return jnp.stack([
            (y_hi if kind is own else 1 - y_hi) * WALL_Z + lax.rem(z + d + WALL_Z, WALL_Z) for kind, d in names
        ]).astype(jnp.int32)

    def add(names, acc, last=False):
        return product([kind[d] for kind, d in names], walls_of(names), here, pattern, coupling, acc, last)

    own[-1], own[1], other[0] = up(own[0]), down(own[0]), across(own[0])
    acc = add([(own, 0)], None)
    own[-2], own[2], other[1] = up(own[-1]), down(own[1]), across(own[1])
    acc = add([(own, -1), (own, 1), (other, 0)], acc)
    own[-3], own[3], other[-2] = up(own[-2]), down(own[2]), across(own[-2])
    acc = add([(own, -2), (own, 2), (other, 1)], acc)
    other[-1], other[2], other[-3] = up(other[0]), down(other[1]), across(own[-3])
    acc = add([(own, -3), (own, 3), (other, -2)], acc)
    other[4], own[4], other[3] = up(other[-3]), down(own[3]), across(own[3])
    acc = add([(other, -1), (other, 2), (other, -3)], acc)
    result = add([(other, 4), (own, 4), (other, 3)], acc, last=True)

    back = lax.all_to_all(result, "mode", 0, 0, axis_index_groups=GROUPS, tiled=True)
    return small_call(unpack_kernel, flip, back, vectors.shape)


def solution(mesh):
    placed = (P(None, "wall", "mode"), P(None, None, "wall", None), P())
    return jax.shard_map(
        per_device, mesh=mesh, in_specs=placed, out_specs=P(None, "wall", "mode"), check_vma=False
    )
```

time: 390 us -> 92 us (0.24)
  waiting for transfers between devices: 313 us -> 13.8 us
  matrix products: 46.1 us -> 0 us
  Pallas kernels: 0 us -> 32.4 us
  blocking collectives: 0 us -> 24.8 us
  between operations: 13.6 us -> 0.15 us
  starting transfers between devices: 6.25 us -> 19.2 us
  other arithmetic: 8.07 us -> 0.38 us
    ppermute x4 -> x15, waiting for transfers between devices: 202 us -> 13.8 us  [the longest x5 13.7 us: up(): return lax.ppermute(value, MODE, UP)]
    all_gather x1 -> x0, waiting for transfers between devices: 111 us -> none  [per_device(): gathered = lax.all_gather(vectors, 'wall', axis=1, tiled=True)]
    dot_general x20 -> x0, matrix products: 46.1 us -> none  [the longest x5 12.5 us: product(): jnp.dot(coup_re, block[0], preferred_element_type=jnp.float32)]
    pallas_call x0 -> x8, Pallas kernels: none -> 32.4 us  [the longest x6 31.4 us: product(): pl.pallas_call(functools.partial(product_kernel, blocks, first, last), ou...]
    all_to_all x0 -> x2, blocking collectives: none -> 24.8 us  [the longest x1 12.8 us: per_device(): lax.all_to_all(pieces, 'mode', 0, 0, axis_index_groups=GROUPS, tiled=True)]
    ppermute x4 -> x15, starting transfers between devices: 6.25 us -> 19.2 us  [the longest x5 12 us: down(): return lax.ppermute(value, MODE, DOWN)]
    mul x1 -> x0, other arithmetic: 7.04 us -> none  [per_device(): masked = coupling * grown[:, None].astype(jnp.bfloat16)]
  transfers between devices with their start and end apart: 5 -> 15, of which waited for: 2 -> 3; matrix products, arithmetic and copies ran while one was open for 8% -> 0% of each run, Pallas kernels for 0% -> 28%
where the time goes in v1:
time: 92 us; the launch traced here: 91.7 us
  Pallas kernels  32.4 us (35%)
  blocking collectives  24.8 us (27%)
  starting transfers between devices  19.2 us (21%)
  waiting for transfers between devices  13.8 us (15%)
  local copies, waits for them, and re-layouts  1.05 us (1%)
    pallas_call x6, Pallas kernels, product(): pl.pallas_call(functools.partial(product_kernel, blocks, first, last), ou...  31.4 us
    ppermute x5, waiting for transfers between devices, up(): return lax.ppermute(value, MODE, UP)  13.7 us
    all_to_all x1, blocking collectives, per_device(): lax.all_to_all(pieces, 'mode', 0, 0, axis_index_groups=GROUPS, tiled=True)  12.8 us
    ppermute x5, starting transfers between devices, down(): return lax.ppermute(value, MODE, DOWN)  12 us
    all_to_all x1, blocking collectives, per_device(): lax.all_to_all(result, 'mode', 0, 0, axis_index_groups=GROUPS, tiled=True)  12 us
    ppermute x5, starting transfers between devices, across(): return lax.ppermute(value, MODE, ACROSS)  3.65 us
    ppermute x5, starting transfers between devices, up(): return lax.ppermute(value, MODE, UP)  3.5 us
  transfers between devices with their start and end apart: 15, of which 3 were waited for; matrix products, arithmetic and copies ran while one was open for 0% of the time, Pallas kernels for 28%

profile of v1, /device:TPU:16, one launch (start us, length us, event | category | flops | bytes accessed | tf_op | source)
XLA Modules:
  0.0 91.7 jit_solution(10445274115497520218)
XLA Ops:
  0.0 1.0 %copy-done = bf16[2,160,512]{2,1,0:T(8,128)(2,1)S(1)} copy-done((bf16[2,160,512]{2,1,0:T(8,128)(2,1)S(1)}, bf16[2,160,512]{2,1,0:T(8,128)(2,1)}, u32[]{:S(2)}) %copy-start) | copy-done | bytes 327704
  1.0 0.1 shard_map.37
  1.1 12.8 %all_to_all.10.refs_0_ = bf16[8,160,128]{2,1,0:T(8,128)(2,1)S(1)} all-to-all(bf16[8,160,128]{2,1,0:T(8,128)(2,1)S(1)} %shard_map.37), channel_id=1, replica_groups={{0,32,64,96,128,160,192,224},{16,48,80,112,144,176,208,240},{1,33,65,97..., dimensions={0} | all-to-all | bytes 655360 | tf_op jit(solution)/shard_map/all_to_all | solution.py:187
  14.0 1.9 %collective-permute-start = (bf16[8,160,128]{2,1,0:T(8,128)(2,1)S(1)}, bf16[8,160,128]{2,1,0:T(8,128)(2,1)S(1)}, u32[]{:S(2)}, u32[]{:S(2)}) collective-permute-start(bf16[8,160,128]{2,1,0:T(8,128)(2,1)S(1)} %all_to_all.10.refs_0_), channel_id=1, source_target_pairs={{0,1},{1,2},{2,3},{3,4},{4,5},{5,6},{6,7},{7,0},{8,9},{9,10},{10,1... | collective-permute-start | bytes 983048 | tf_op jit(solution)/shard_map/ppermute | solution.py:48
  15.9 3.9 %collective-permute-start.5 = (bf16[8,160,128]{2,1,0:T(8,128)(2,1)S(1)}, bf16[8,160,128]{2,1,0:T(8,128)(2,1)S(1)}, u32[]{:S(2)}, u32[]{:S(2)}) collective-permute-start(bf16[8,160,128]{2,1,0:T(8,128)(2,1)S(1)} %all_to_all.10.refs_0_), channel_id=1, source_target_pairs={{0,7},{1,0},{2,1},{3,2},{4,3},{5,4},{6,5},{7,6},{8,15},{9,8},{10,9... | collective-permute-start | bytes 983048 | tf_op jit(solution)/shard_map/ppermute | solution.py:52
  19.8 6.3 %collective-permute-done.refs_0_ = bf16[8,160,128]{2,1,0:T(8,128)(2,1)S(1)} collective-permute-done((bf16[8,160,128]{2,1,0:T(8,128)(2,1)S(1)}, bf16[8,160,128]{2,1,0:T(8,128)(2,1)S(1)}, u32[]{:S(2)}, u32[]{:S(2)}) %collective-permute-start) | collective-permute-done | bytes 327712 | tf_op jit(solution)/shard_map/ppermute | solution.py:48
  26.1 0.1 pad_add_fusion.4.walls_ref
  26.1 0.1 pad_add_fusion.3.walls_ref
  26.2 0.1 collective-permute-start.10
  26.3 3.3 %collective-permute-start.6 = (bf16[8,160,128]{2,1,0:T(8,128)(2,1)S(1)}, bf16[8,160,128]{2,1,0:T(8,128)(2,1)S(1)}, u32[]{:S(2)}, u32[]{:S(2)}) collective-permute-start(bf16[8,160,128]{2,1,0:T(8,128)(2,1)S(1)} %collective-permute-done.5.refs_1_), channel_id=1, source_target_pairs={{0,7},{1,0},{2,1},{3,2},{4,3},{5,4},{6,5},{7,6},{8,15},{9,8},{10,9... | collective-permute-start | bytes 983048 | tf_op jit(solution)/shard_map/ppermute | solution.py:52
  29.6 5.1 %collective-permute-done.1.refs_0_ = bf16[8,160,128]{2,1,0:T(8,128)(2,1)S(1)} collective-permute-done((bf16[8,160,128]{2,1,0:T(8,128)(2,1)S(1)}, bf16[8,160,128]{2,1,0:T(8,128)(2,1)S(1)}, u32[]{:S(2)}, u32[]{:S(2)}) %collective-permute-start.1) | collective-permute-done | bytes 327712 | tf_op jit(solution)/shard_map/ppermute | solution.py:48
  34.6 0.1 pad_add_fusion.2.walls_ref
  34.7 0.1 pad_add_fusion.1.walls_ref
  34.8 0.1 collective-permute-start.12
  34.9 0.1 pad_add_fusion.walls_ref
  35.0 0.1 reshape.11.pattern_ref
  35.0 2.9 %shard_map.38.refs_5_ = f32[8,320,128]{2,1,0:T(8,128)S(1)} custom-call(s32[1]{0:T(128)} %bitcast.17.walls_ref, s32[1]{0:T(128)} %bitcast.4.here_ref, s32[1280]{0:T(1024)S(1)} %reshape.11.pattern_ref, bf16[8,160,128]{2,1,0:T(8,128)(2,1)S(1)} %all_to_all.10.refs_0_, bf16[5,2,160,2560]{3,2,1,0:T(8,128)(2,1)} %refs_4_.9, bf16[5,2,160,2560]{3,2,1,0:T(8,128)(2,1)} %refs_4_.9), custom_call_target="tpu_custom_call" | custom-call | flops 838860800 | bytes 3800000 | tf_op jit(solution)/shard_map/pallas_call | solution.py:168
  38.0 0.1 collective-permute-start.11
  38.1 2.0 %collective-permute-start.14 = (bf16[8,160,128]{2,1,0:T(8,128)(2,1)S(1)}, bf16[8,160,128]{2,1,0:T(8,128)(2,1)S(1)}, u32[]{:S(2)}, u32[]{:S(2)}) collective-permute-start(bf16[8,160,128]{2,1,0:T(8,128)(2,1)S(1)} %collective-permute-done.1.refs_0_), channel_id=1, source_target_pairs={{0,40},{1,41},{2,42},{3,43},{4,44},{5,45},{6,46},{7,47},{8,32},{9,... | collective-permute-start | bytes 983048 | tf_op jit(solution)/shard_map/ppermute | solution.py:56
  40.1 3.2 %collective-permute-start.7 = (bf16[8,160,128]{2,1,0:T(8,128)(2,1)S(1)}, bf16[8,160,128]{2,1,0:T(8,128)(2,1)S(1)}, u32[]{:S(2)}, u32[]{:S(2)}) collective-permute-start(bf16[8,160,128]{2,1,0:T(8,128)(2,1)S(1)} %collective-permute-done.6.refs_1_), channel_id=1, source_target_pairs={{0,7},{1,0},{2,1},{3,2},{4,3},{5,4},{6,5},{7,6},{8,15},{9,8},{10,9... | collective-permute-start | bytes 983048 | tf_op jit(solution)/shard_map/ppermute | solution.py:52
  43.4 2.4 %collective-permute-done.2.refs_0_ = bf16[8,160,128]{2,1,0:T(8,128)(2,1)S(1)} collective-permute-done((bf16[8,160,128]{2,1,0:T(8,128)(2,1)S(1)}, bf16[8,160,128]{2,1,0:T(8,128)(2,1)S(1)}, u32[]{:S(2)}, u32[]{:S(2)}) %collective-permute-start.2) | collective-permute-done | bytes 327712 | tf_op jit(solution)/shard_map/ppermute | solution.py:48
  45.8 5.6 %shard_map.39.refs_5_ = f32[8,320,128]{2,1,0:T(8,128)S(1)} custom-call(s32[3]{0:T(128)S(1)} %pad_add_fusion.4.walls_ref, s32[1]{0:T(128)} %bitcast.4.here_ref, s32[1280]{0:T(1024)S(1)} %reshape.11.pattern_ref, bf16[8,160,128]{2,1,0:T(8,128)(2,1)S(1)} %collective-permute-done.refs_0_, bf16[8,160,128]{2,1,0:T(8,128)(2,1)S(1)} %collective-permute-done.5.refs_1_, ...), custom_call_target="tpu_custom_call" | custom-call | flops 2516582400 | bytes 6200000 | tf_op jit(solution)/shard_map/pallas_call | solution.py:168
  51.5 0.1 collective-permute-start.13
  51.5 5.6 %shard_map.40.refs_5_ = f32[8,320,128]{2,1,0:T(8,128)S(1)} custom-call(s32[3]{0:T(128)S(1)} %pad_add_fusion.3.walls_ref, s32[1]{0:T(128)} %bitcast.4.here_ref, s32[1280]{0:T(1024)S(1)} %reshape.11.pattern_ref, bf16[8,160,128]{2,1,0:T(8,128)(2,1)S(1)} %collective-permute-done.1.refs_0_, bf16[8,160,128]{2,1,0:T(8,128)(2,1)S(1)} %collective-permute-done.6.refs_1_, ...), custom_call_target="tpu_custom_call" | custom-call | flops 2516582400 | bytes 6200000 | tf_op jit(solution)/shard_map/pallas_call | solution.py:168
  57.2 1.4 %collective-permute-start.8 = (bf16[8,160,128]{2,1,0:T(8,128)(2,1)S(1)}, bf16[8,160,128]{2,1,0:T(8,128)(2,1)S(1)}, u32[]{:S(2)}, u32[]{:S(2)}) collective-permute-start(bf16[8,160,128]{2,1,0:T(8,128)(2,1)S(1)} %collective-permute-done.7.refs_1_), channel_id=1, source_target_pairs={{0,7},{1,0},{2,1},{3,2},{4,3},{5,4},{6,5},{7,6},{8,15},{9,8},{10,9... | collective-permute-start | bytes 983048 | tf_op jit(solution)/shard_map/ppermute | solution.py:52
  58.7 1.4 %collective-permute-start.9 = (bf16[8,160,128]{2,1,0:T(8,128)(2,1)S(1)}, bf16[8,160,128]{2,1,0:T(8,128)(2,1)S(1)}, u32[]{:S(2)}, u32[]{:S(2)}) collective-permute-start(bf16[8,160,128]{2,1,0:T(8,128)(2,1)S(1)} %collective-permute-done.7.refs_1_), channel_id=1, source_target_pairs={{0,40},{1,41},{2,42},{3,43},{4,44},{5,45},{6,46},{7,47},{8,32},{9,... | collective-permute-start | bytes 983048 | tf_op jit(solution)/shard_map/ppermute | solution.py:56
  60.1 1.5 %collective-permute-start.4 = (bf16[8,160,128]{2,1,0:T(8,128)(2,1)S(1)}, bf16[8,160,128]{2,1,0:T(8,128)(2,1)S(1)}, u32[]{:S(2)}, u32[]{:S(2)}) collective-permute-start(bf16[8,160,128]{2,1,0:T(8,128)(2,1)S(1)} %collective-permute-done.3.refs_2_), channel_id=1, source_target_pairs={{0,1},{1,2},{2,3},{3,4},{4,5},{5,6},{6,7},{7,0},{8,9},{9,10},{10,1... | collective-permute-start | bytes 983048 | tf_op jit(solution)/shard_map/ppermute | solution.py:48
  61.6 5.6 %shard_map.41.refs_5_ = f32[8,320,128]{2,1,0:T(8,128)S(1)} custom-call(s32[3]{0:T(128)S(1)} %pad_add_fusion.2.walls_ref, s32[1]{0:T(128)} %bitcast.4.here_ref, s32[1280]{0:T(1024)S(1)} %reshape.11.pattern_ref, bf16[8,160,128]{2,1,0:T(8,128)(2,1)S(1)} %collective-permute-done.2.refs_0_, bf16[8,160,128]{2,1,0:T(8,128)(2,1)S(1)} %collective-permute-done.7.refs_1_, ...), custom_call_target="tpu_custom_call" | custom-call | flops 2516582400 | bytes 6200000 | tf_op jit(solution)/shard_map/pallas_call | solution.py:168
  67.3 5.6 %shard_map.42.refs_5_ = f32[8,320,128]{2,1,0:T(8,128)S(1)} custom-call(s32[3]{0:T(128)S(1)} %pad_add_fusion.1.walls_ref, s32[1]{0:T(128)} %bitcast.4.here_ref, s32[1280]{0:T(1024)S(1)} %reshape.11.pattern_ref, bf16[8,160,128]{2,1,0:T(8,128)(2,1)S(1)} %collective-permute-done.11.refs_0_, bf16[8,160,128]{2,1,0:T(8,128)(2,1)S(1)} %collective-permute-done.13.refs_1_, ...), custom_call_target="tpu_custom_call" | custom-call | flops 2516582400 | bytes 6200000 | tf_op jit(solution)/shard_map/pallas_call | solution.py:168
  73.0 5.9 %shard_map.43 = bf16[8,160,128]{2,1,0:T(8,128)(2,1)S(1)} custom-call(s32[3]{0:T(128)S(1)} %pad_add_fusion.walls_ref, s32[1]{0:T(128)} %bitcast.4.here_ref, s32[1280]{0:T(1024)S(1)} %reshape.11.pattern_ref, bf16[8,160,128]{2,1,0:T(8,128)(2,1)S(1)} %collective-permute-done.4.refs_0_, bf16[8,160,128]{2,1,0:T(8,128)(2,1)S(1)} %collective-permute-done.8.refs_1_, ...), custom_call_target="tpu_custom_call" | custom-call | flops 2516582400 | bytes 6200000 | tf_op jit(solution)/shard_map/pallas_call | solution.py:168
  78.8 12.0 %all_to_all.11.pieces_ref = bf16[8,160,128]{2,1,0:T(8,128)(2,1)S(1)} all-to-all(bf16[8,160,128]{2,1,0:T(8,128)(2,1)S(1)} %shard_map.43), channel_id=1, replica_groups={{0,32,64,96,128,160,192,224},{16,48,80,112,144,176,208,240},{1,33,65,97..., dimensions={0} | all-to-all | bytes 655360 | tf_op jit(solution)/shard_map/all_to_all | solution.py:211
  90.8 0.9 shard_map.44
  (18 shorter events, 0.0 us)
Async XLA Ops:
  0.0 1.0 %copy-start = (bf16[2,160,512]{2,1,0:T(8,128)(2,1)S(1)}, bf16[2,160,512]{2,1,0:T(8,128)(2,1)}, u32[]{:S(2)}) copy-start(bf16[2,160,512]{2,1,0:T(8,128)(2,1)} %x_ref.1) | copy-start | bytes 983044
  1.0 34.0 %copy-start.1 = (s32[5,16,16]{2,1,0:T(8,128)S(1)}, s32[5,16,16]{2,1,0:T(8,128)}, u32[]{:S(2)}) copy-start(s32[5,16,16]{2,1,0:T(8,128)} %param.5) | copy-start | bytes 15364
  14.0 12.1 %collective-permute-start = (bf16[8,160,128]{2,1,0:T(8,128)(2,1)S(1)}, bf16[8,160,128]{2,1,0:T(8,128)(2,1)S(1)}, u32[]{:S(2)}, u32[]{:S(2)}) collective-permute-start(bf16[8,160,128]{2,1,0:T(8,128)(2,1)S(1)} %all_to_all.10.refs_0_), channel_id=1, source_target_pairs={{0,1},{1,2},{2,3},{3,4},{4,5},{5,6},{6,7},{7,0},{8,9},{9,10},{10,1... | collective-permute-start | bytes 983048 | tf_op jit(solution)/shard_map/ppermute | solution.py:48
  15.9 10.4 %collective-permute-start.5 = (bf16[8,160,128]{2,1,0:T(8,128)(2,1)S(1)}, bf16[8,160,128]{2,1,0:T(8,128)(2,1)S(1)}, u32[]{:S(2)}, u32[]{:S(2)}) collective-permute-start(bf16[8,160,128]{2,1,0:T(8,128)(2,1)S(1)} %all_to_all.10.refs_0_), channel_id=1, source_target_pairs={{0,7},{1,0},{2,1},{3,2},{4,3},{5,4},{6,5},{7,6},{8,15},{9,8},{10,9... | collective-permute-start | bytes 983048 | tf_op jit(solution)/shard_map/ppermute | solution.py:52
  26.1 8.6 %collective-permute-start.1 = (bf16[8,160,128]{2,1,0:T(8,128)(2,1)S(1)}, bf16[8,160,128]{2,1,0:T(8,128)(2,1)S(1)}, u32[]{:S(2)}, u32[]{:S(2)}) collective-permute-start(bf16[8,160,128]{2,1,0:T(8,128)(2,1)S(1)} %collective-permute-done.refs_0_), channel_id=1, source_target_pairs={{0,1},{1,2},{2,3},{3,4},{4,5},{5,6},{6,7},{7,0},{8,9},{9,10},{10,1... | collective-permute-start | bytes 983048 | tf_op jit(solution)/shard_map/ppermute | solution.py:48
  26.2 11.8 %collective-permute-start.10 = (bf16[8,160,128]{2,1,0:T(8,128)(2,1)S(1)}, bf16[8,160,128]{2,1,0:T(8,128)(2,1)S(1)}, u32[]{:S(2)}, u32[]{:S(2)}) collective-permute-start(bf16[8,160,128]{2,1,0:T(8,128)(2,1)S(1)} %all_to_all.10.refs_0_), channel_id=1, source_target_pairs={{0,40},{1,41},{2,42},{3,43},{4,44},{5,45},{6,46},{7,47},{8,32},{9,... | collective-permute-start | bytes 983048 | tf_op jit(solution)/shard_map/ppermute | solution.py:56
  26.3 13.8 %collective-permute-start.6 = (bf16[8,160,128]{2,1,0:T(8,128)(2,1)S(1)}, bf16[8,160,128]{2,1,0:T(8,128)(2,1)S(1)}, u32[]{:S(2)}, u32[]{:S(2)}) collective-permute-start(bf16[8,160,128]{2,1,0:T(8,128)(2,1)S(1)} %collective-permute-done.5.refs_1_), channel_id=1, source_target_pairs={{0,7},{1,0},{2,1},{3,2},{4,3},{5,4},{6,5},{7,6},{8,15},{9,8},{10,9... | collective-permute-start | bytes 983048 | tf_op jit(solution)/shard_map/ppermute | solution.py:52
  34.6 11.2 %collective-permute-start.2 = (bf16[8,160,128]{2,1,0:T(8,128)(2,1)S(1)}, bf16[8,160,128]{2,1,0:T(8,128)(2,1)S(1)}, u32[]{:S(2)}, u32[]{:S(2)}) collective-permute-start(bf16[8,160,128]{2,1,0:T(8,128)(2,1)S(1)} %collective-permute-done.1.refs_0_), channel_id=1, source_target_pairs={{0,1},{1,2},{2,3},{3,4},{4,5},{5,6},{6,7},{7,0},{8,9},{9,10},{10,1... | collective-permute-start | bytes 983048 | tf_op jit(solution)/shard_map/ppermute | solution.py:48
  34.8 16.7 %collective-permute-start.12 = (bf16[8,160,128]{2,1,0:T(8,128)(2,1)S(1)}, bf16[8,160,128]{2,1,0:T(8,128)(2,1)S(1)}, u32[]{:S(2)}, u32[]{:S(2)}) collective-permute-start(bf16[8,160,128]{2,1,0:T(8,128)(2,1)S(1)} %collective-permute-done.5.refs_1_), channel_id=1, source_target_pairs={{0,40},{1,41},{2,42},{3,43},{4,44},{5,45},{6,46},{7,47},{8,32},{9,... | collective-permute-start | bytes 983048 | tf_op jit(solution)/shard_map/ppermute | solution.py:56
  38.0 29.3 %collective-permute-start.11 = (bf16[8,160,128]{2,1,0:T(8,128)(2,1)S(1)}, bf16[8,160,128]{2,1,0:T(8,128)(2,1)S(1)}, u32[]{:S(2)}, u32[]{:S(2)}) collective-permute-start(bf16[8,160,128]{2,1,0:T(8,128)(2,1)S(1)} %collective-permute-done.10.refs_2_), channel_id=1, source_target_pairs={{0,1},{1,2},{2,3},{3,4},{4,5},{5,6},{6,7},{7,0},{8,9},{9,10},{10,1... | collective-permute-start | bytes 983048 | tf_op jit(solution)/shard_map/ppermute | solution.py:48
  38.1 20.6 %collective-permute-start.14 = (bf16[8,160,128]{2,1,0:T(8,128)(2,1)S(1)}, bf16[8,160,128]{2,1,0:T(8,128)(2,1)S(1)}, u32[]{:S(2)}, u32[]{:S(2)}) collective-permute-start(bf16[8,160,128]{2,1,0:T(8,128)(2,1)S(1)} %collective-permute-done.1.refs_0_), channel_id=1, source_target_pairs={{0,40},{1,41},{2,42},{3,43},{4,44},{5,45},{6,46},{7,47},{8,32},{9,... | collective-permute-start | bytes 983048 | tf_op jit(solution)/shard_map/ppermute | solution.py:56
  40.1 17.1 %collective-permute-start.7 = (bf16[8,160,128]{2,1,0:T(8,128)(2,1)S(1)}, bf16[8,160,128]{2,1,0:T(8,128)(2,1)S(1)}, u32[]{:S(2)}, u32[]{:S(2)}) collective-permute-start(bf16[8,160,128]{2,1,0:T(8,128)(2,1)S(1)} %collective-permute-done.6.refs_1_), channel_id=1, source_target_pairs={{0,7},{1,0},{2,1},{3,2},{4,3},{5,4},{6,5},{7,6},{8,15},{9,8},{10,9... | collective-permute-start | bytes 983048 | tf_op jit(solution)/shard_map/ppermute | solution.py:52
  45.8 14.3 %collective-permute-start.3 = (bf16[8,160,128]{2,1,0:T(8,128)(2,1)S(1)}, bf16[8,160,128]{2,1,0:T(8,128)(2,1)S(1)}, u32[]{:S(2)}, u32[]{:S(2)}) collective-permute-start(bf16[8,160,128]{2,1,0:T(8,128)(2,1)S(1)} %collective-permute-done.2.refs_0_), channel_id=1, source_target_pairs={{0,40},{1,41},{2,42},{3,43},{4,44},{5,45},{6,46},{7,47},{8,32},{9,... | collective-permute-start | bytes 983048 | tf_op jit(solution)/shard_map/ppermute | solution.py:56
  51.5 15.8 %collective-permute-start.13 = (bf16[8,160,128]{2,1,0:T(8,128)(2,1)S(1)}, bf16[8,160,128]{2,1,0:T(8,128)(2,1)S(1)}, u32[]{:S(2)}, u32[]{:S(2)}) collective-permute-start(bf16[8,160,128]{2,1,0:T(8,128)(2,1)S(1)} %collective-permute-done.12.refs_2_), channel_id=1, source_target_pairs={{0,7},{1,0},{2,1},{3,2},{4,3},{5,4},{6,5},{7,6},{8,15},{9,8},{10,9... | collective-permute-start | bytes 983048 | tf_op jit(solution)/shard_map/ppermute | solution.py:52
  57.2 15.7 %collective-permute-start.8 = (bf16[8,160,128]{2,1,0:T(8,128)(2,1)S(1)}, bf16[8,160,128]{2,1,0:T(8,128)(2,1)S(1)}, u32[]{:S(2)}, u32[]{:S(2)}) collective-permute-start(bf16[8,160,128]{2,1,0:T(8,128)(2,1)S(1)} %collective-permute-done.7.refs_1_), channel_id=1, source_target_pairs={{0,7},{1,0},{2,1},{3,2},{4,3},{5,4},{6,5},{7,6},{8,15},{9,8},{10,9... | collective-permute-start | bytes 983048 | tf_op jit(solution)/shard_map/ppermute | solution.py:52
  58.7 14.3 %collective-permute-start.9 = (bf16[8,160,128]{2,1,0:T(8,128)(2,1)S(1)}, bf16[8,160,128]{2,1,0:T(8,128)(2,1)S(1)}, u32[]{:S(2)}, u32[]{:S(2)}) collective-permute-start(bf16[8,160,128]{2,1,0:T(8,128)(2,1)S(1)} %collective-permute-done.7.refs_1_), channel_id=1, source_target_pairs={{0,40},{1,41},{2,42},{3,43},{4,44},{5,45},{6,46},{7,47},{8,32},{9,... | collective-permute-start | bytes 983048 | tf_op jit(solution)/shard_map/ppermute | solution.py:56
  60.1 12.8 %collective-permute-start.4 = (bf16[8,160,128]{2,1,0:T(8,128)(2,1)S(1)}, bf16[8,160,128]{2,1,0:T(8,128)(2,1)S(1)}, u32[]{:S(2)}, u32[]{:S(2)}) collective-permute-start(bf16[8,160,128]{2,1,0:T(8,128)(2,1)S(1)} %collective-permute-done.3.refs_2_), channel_id=1, source_target_pairs={{0,1},{1,2},{2,3},{3,4},{4,5},{5,6},{6,7},{7,0},{8,9},{9,10},{10,1... | collective-permute-start | bytes 983048 | tf_op jit(solution)/shard_map/ppermute | solution.py:48

commit v2 on v1

v2 whole, which is shorter than its diff:
```python
import functools

import jax
import jax.numpy as jnp
from jax import lax
from jax.experimental import pallas as pl
from jax.experimental.pallas import tpu as pltpu
from jax.sharding import PartitionSpec as P

F = 5
BLK = 32
ROWS = F * BLK
HMAX = 2
NOFF = 2 * HMAX + 1
Q = 8
HALF = 64
TILE = 2 * HALF
CORES = 2
WALL_Z = 8
WALLS = 16
RUN = 4
WINDOW = 768
HALF_TILES = 10
RING_TILES = 14
VMEM_BYTES = 24 * 2**20

MODE = ("mode", "wall")
GROUPS = [[2 * q + core for q in range(Q)] for core in range(CORES)]


def permutation(move):
    pairs = []
    for x in range(4):
        for y_lo in range(2):
            for core in range(CORES):
                for y_hi in range(2):
                    for z in range(WALL_Z):
                        nx, ny_lo, ny_hi, nz = move(x, y_lo, y_hi, z)
                        pairs.append((
                            ((x * 2 + y_lo) * CORES + core) * 16 + y_hi * WALL_Z + z,
                            ((nx * 2 + ny_lo) * CORES + core) * 16 + ny_hi * WALL_Z + nz,
                        ))
    return pairs


UP = permutation(lambda x, y_lo, y_hi, z: (x, y_lo, y_hi, (z + 1) % WALL_Z))
DOWN = permutation(lambda x, y_lo, y_hi, z: (x, y_lo, y_hi, (z - 1) % WALL_Z))
ACROSS = permutation(lambda x, y_lo, y_hi, z: (x, 1 - y_lo, 1 - y_hi, z))
ACROSS_DOWN = permutation(lambda x, y_lo, y_hi, z: (x, 1 - y_lo, 1 - y_hi, (z - 1) % WALL_Z))


def up(value):
    return lax.ppermute(value, MODE, UP)


def down(value):
    return lax.ppermute(value, MODE, DOWN)


def across(value):
    return lax.ppermute(value, MODE, ACROSS)


def across_down(value):
    return lax.ppermute(value, MODE, ACROSS_DOWN)


def pack_kernel(flip_ref, x_ref, out_ref):
    flip = flip_ref[0]
    for c in range(Q):
        cols = slice(c * HALF, (c + 1) * HALF)
        out_ref[c ^ flip] = jnp.concatenate([x_ref[0, :, cols], x_ref[1, :, cols]], axis=1)


def unpack_kernel(flip_ref, pieces_ref, out_ref):
    flip = flip_ref[0]
    for t in range(Q // 2):
        a = pieces_ref[(2 * t) ^ flip]
        b = pieces_ref[(2 * t + 1) ^ flip]
        cols = slice(t * TILE, (t + 1) * TILE)
        out_ref[0, :, cols] = jnp.concatenate([a[:, :HALF], b[:, :HALF]], axis=1)
        out_ref[1, :, cols] = jnp.concatenate([a[:, HALF:], b[:, HALF:]], axis=1)


def small_call(kernel, flip, value, shape):
    return pl.pallas_call(
        kernel,
        out_shape=jax.ShapeDtypeStruct(shape, value.dtype),
        in_specs=[pl.BlockSpec(memory_space=pltpu.SMEM), pl.BlockSpec(memory_space=pltpu.VMEM)],
        out_specs=pl.BlockSpec(memory_space=pltpu.VMEM),
        compiler_params=pltpu.CompilerParams(vmem_limit_bytes=VMEM_BYTES),
        cost_estimate=pl.CostEstimate(flops=0, bytes_accessed=4 * value.size, transcendentals=0),
    )(flip, value)


def mask_kernel(here_ref, pattern_ref, e_ref, out_ref, held_ref, sems):
    here = here_ref[0]
    lane = lax.broadcasted_iota(jnp.int32, (1, 128), 1)
    copies = [pltpu.make_async_copy(e_ref.at[h], held_ref.at[h], sems.at[h]) for h in range(NOFF)]
    for copy in copies:
        copy.start()
    for h in range(NOFF):
        copies[h].wait()
        for t in range(WALLS * ROWS // 128):
            low = t * 128 // ROWS
            high = (t * 128 + 127) // ROWS
            present = pattern_ref[(h * WALLS + low) * WALLS + here]
            if high > low:
                after = pattern_ref[(h * WALLS + high) * WALLS + here]
                present = jnp.where(lane < high * ROWS - t * 128, present, after)
            else:
                present = jnp.broadcast_to(present, (1, 128))
            mask = present.astype(jnp.float32).astype(jnp.bfloat16)
            half, at = t // HALF_TILES, t % HALF_TILES
            for part in range(2):
                value = held_ref[h, part, :, t * 128:(t + 1) * 128] * mask
                out_ref[half, h, part, :, at * 128:(at + 1) * 128] = value
                if at + HALF_TILES < RING_TILES:
                    out_ref[half, h, part, :, (at + HALF_TILES) * 128:(at + HALF_TILES + 1) * 128] = value


def masked_ring(here, pattern, coupling):
    smem = pl.BlockSpec(memory_space=pltpu.SMEM)
    return pl.pallas_call(
        mask_kernel,
        out_shape=jax.ShapeDtypeStruct((2, NOFF, 2, ROWS, RING_TILES * 128), coupling.dtype),
        in_specs=[smem, smem, pl.BlockSpec(memory_space=pltpu.HBM)],
        out_specs=pl.BlockSpec(memory_space=pltpu.VMEM),
        scratch_shapes=[pltpu.VMEM(coupling.shape, coupling.dtype), pltpu.SemaphoreType.DMA((NOFF,))],
        compiler_params=pltpu.CompilerParams(vmem_limit_bytes=VMEM_BYTES),
        cost_estimate=pl.CostEstimate(flops=0, bytes_accessed=8 * 2**20, transcendentals=0),
    )(here, pattern, pltpu.with_memory_space_constraint(coupling, pltpu.HBM))


def run_kernel(far, start, first, last, here_ref, e_ref, *refs):
    x_refs, rest = refs[:RUN], refs[RUN:]
    if first:
        out_ref, padded_ref = rest
    else:
        acc_ref, out_ref, padded_ref = rest
    here = here_ref[0]
    y_hi, z = here // WALL_Z, lax.rem(here, WALL_Z)
    half = 1 - y_hi if far else y_hi
    begin = lax.rem(z + start + WALL_Z, WALL_Z)
    offset = pl.multiple_of(lax.rem(begin, 4) * 32, 32)
    lanes = pl.multiple_of(begin * 5 // 4 * 128, 128)
    padded_ref[:, :128, :] = jnp.zeros((Q, 128, TILE), jnp.bfloat16)
    padded_ref[:, WINDOW - 128:, :] = jnp.zeros((Q, 128, TILE), jnp.bfloat16)
    for j in range(RUN):
        padded_ref[:, pl.ds(pl.multiple_of(offset + j * ROWS, 32), ROWS), :] = x_refs[j][...]
    left = jnp.concatenate(
        [
            jnp.concatenate([e_ref[half, h, part, :, pl.ds(lanes, WINDOW)] for h in range(NOFF)], axis=1)
            for part in range(2)
        ],
        axis=0,
    )
    lane = lax.broadcasted_iota(jnp.int32, (ROWS, TILE), 1)
    for pair in range(Q // 2):
        q = 2 * pair
        right = jnp.concatenate(
            [
                jnp.concatenate([padded_ref[(q + k - (h - HMAX)) % Q] for k in range(2)], axis=1)
                for h in range(NOFF)
            ],
            axis=0,
        )
        result = jnp.dot(left, right, preferred_element_type=jnp.float32)
        for k in range(2):
            part = result[:, k * TILE:(k + 1) * TILE]
            if not first:
                part = acc_ref[q + k] + part
            if last:
                turned = pltpu.roll(part[ROWS:], HALF, 1)
                part = (part[:ROWS] + jnp.where(lane < HALF, -turned, turned)).astype(out_ref.dtype)
            out_ref[q + k] = part


def run_product(xs, far, start, here, ring, acc, last=False):
    first = acc is None
    vmem, smem = pl.BlockSpec(memory_space=pltpu.VMEM), pl.BlockSpec(memory_space=pltpu.SMEM)
    operands = [here, ring, *xs] + ([] if first else [acc])
    if last:
        out_shape = jax.ShapeDtypeStruct((Q, ROWS, TILE), jnp.bfloat16)
    else:
        out_shape = jax.ShapeDtypeStruct((Q, 2 * ROWS, TILE), jnp.float32)
    return pl.pallas_call(
        functools.partial(run_kernel, far, start, first, last),
        out_shape=out_shape,
        in_specs=[smem] + [vmem] * (len(operands) - 1),
        out_specs=vmem,
        scratch_shapes=[pltpu.VMEM((Q, WINDOW, TILE), jnp.bfloat16)],
        compiler_params=pltpu.CompilerParams(vmem_limit_bytes=VMEM_BYTES),
        cost_estimate=pl.CostEstimate(
            flops=2 * NOFF * WINDOW * 2 * ROWS * Q * TILE, bytes_accessed=3 * 2**20, transcendentals=0
        ),
    )(*operands)


def per_device(vectors, coupling, pattern):
    wall = lax.axis_index("wall")
    flip = (wall // WALL_Z).reshape(1).astype(jnp.int32)
    here = wall.reshape(1).astype(jnp.int32)
    pattern = pattern.reshape(-1)
    tie = lax.optimization_barrier

    pieces = small_call(pack_kernel, flip, vectors, (Q, ROWS, TILE))
    block = lax.all_to_all(pieces, "mode", 0, 0, axis_index_groups=GROUPS, tiled=True)

    own, other = {0: block}, {}

    def add(far, start, acc, last=False):
        kind = other if far else own
        xs = [kind[(start + j + 3) % WALL_Z - 3] for j in range(RUN)]
        return run_product(xs, far, start, here, ring, acc, last)

    own[1], own[-1], other[0] = down(own[0]), up(own[0]), across(own[0])
    ring = masked_ring(here, pattern, coupling)
    own[1], ring = tie((own[1], ring))
    own[2], other[1] = down(own[1]), across(own[1])
    own[-1], other[0] = tie((own[-1], other[0]))
    own[-2] = up(own[-1])
    own[3] = down(own[2])
    other[-2] = across(own[-2])
    own[-2], other[1] = tie((own[-2], other[1]))
    own[-3] = up(own[-2])
    other[-1] = up(other[0])
    other[2] = down(other[1])
    acc = add(0, -2, None)
    own[3], acc = tie((own[3], acc))
    own[4], other[3], other[4] = down(own[3]), across(own[3]), across_down(own[3])
    other[-3] = up(other[-2])
    acc = add(1, -2, acc)
    acc = add(0, 2, acc)
    result = add(1, 2, acc, last=True)

    back = lax.all_to_all(result, "mode", 0, 0, axis_index_groups=GROUPS, tiled=True)
    return small_call(unpack_kernel, flip, back, vectors.shape)


def solution(mesh):
    placed = (P(None, "wall", "mode"), P(None, None, "wall", None), P())
    return jax.shard_map(
        per_device, mesh=mesh, in_specs=placed, out_specs=P(None, "wall", "mode"), check_vma=False
    )
```

time: 92 us -> 78.6 us (0.85)
  Pallas kernels: 32.4 us -> 17 us
  starting transfers between devices: 19.2 us -> 23.4 us
  waiting for transfers between devices: 13.8 us -> 12.5 us
    pallas_call x6 -> x5, Pallas kernels: 31.4 us -> 15.9 us  [the longest x4 11.5 us: run_product(): pl.pallas_call(functools.partial(run_kernel, far, start, first, last), ou...]
    ppermute x5, waiting for transfers between devices: 13.7 us -> 2.98 us  [up(): return lax.ppermute(value, MODE, UP)]
    ppermute x5, waiting for transfers between devices: 0.01 us -> 6.03 us  [down(): return lax.ppermute(value, MODE, DOWN)]
    ppermute x5, starting transfers between devices: 12 us -> 16.8 us  [down(): return lax.ppermute(value, MODE, DOWN)]
    ppermute x0 -> x1, waiting for transfers between devices: none -> 3.51 us  [across_down(): return lax.ppermute(value, MODE, ACROSS_DOWN)]
    ppermute x5, starting transfers between devices: 3.5 us -> 0.01 us  [up(): return lax.ppermute(value, MODE, UP)]
    ppermute x0 -> x1, starting transfers between devices: none -> 2.78 us  [across_down(): return lax.ppermute(value, MODE, ACROSS_DOWN)]
    ppermute x5 -> x4, starting transfers between devices: 3.65 us -> 3.81 us  [across(): return lax.ppermute(value, MODE, ACROSS)]
  transfers between devices with their start and end apart: 15 -> 15, of which waited for: 3 -> 6; matrix products, arithmetic and copies ran while one was open for 0% -> 0% of each run, Pallas kernels for 28% -> 16%
where the time goes in v2:
time: 78.6 us; the launch traced here: 78.4 us
  blocking collectives  24.4 us (31%)
  starting transfers between devices  23.4 us (30%)
  Pallas kernels  17 us (22%)
  waiting for transfers between devices  12.5 us (16%)
  local copies, waits for them, and re-layouts  1.05 us (1%)
    ppermute x5, starting transfers between devices, down(): return lax.ppermute(value, MODE, DOWN)  16.8 us
    all_to_all x1, blocking collectives, per_device(): lax.all_to_all(pieces, 'mode', 0, 0, axis_index_groups=GROUPS, tiled=True)  12.8 us
    all_to_all x1, blocking collectives, per_device(): lax.all_to_all(result, 'mode', 0, 0, axis_index_groups=GROUPS, tiled=True)  11.6 us
    pallas_call x4, Pallas kernels, run_product(): pl.pallas_call(functools.partial(run_kernel, far, start, first, last), ou...  11.5 us
    ppermute x5, waiting for transfers between devices, down(): return lax.ppermute(value, MODE, DOWN)  6.03 us
    pallas_call x1, Pallas kernels, masked_ring(): pl.pallas_call(mask_kernel, out_shape=jax.ShapeDtypeStruct((2, NOFF, 2, R...  4.39 us
    ppermute x4, starting transfers between devices, across(): return lax.ppermute(value, MODE, ACROSS)  3.81 us
    ppermute x1, waiting for transfers between devices, across_down(): return lax.ppermute(value, MODE, ACROSS_DOWN)  3.51 us
  transfers between devices with their start and end apart: 15, of which 6 were waited for; matrix products, arithmetic and copies ran while one was open for 0% of the time, Pallas kernels for 16%

profile of v2, /device:TPU:16, one launch (start us, length us, event | category | flops | bytes accessed | tf_op | source)
XLA Modules:
  0.0 78.4 jit_solution(10518243158821974280)
XLA Ops:
  0.0 1.0 %copy-done = bf16[2,160,512]{2,1,0:T(8,128)(2,1)S(1)} copy-done((bf16[2,160,512]{2,1,0:T(8,128)(2,1)S(1)}, bf16[2,160,512]{2,1,0:T(8,128)(2,1)}, u32[]{:S(2)}) %copy-start) | copy-done | bytes 327704
  1.0 0.1 shard_map.37
  1.1 12.8 %all_to_all.10.refs_2_ = bf16[8,160,128]{2,1,0:T(8,128)(2,1)S(1)} all-to-all(bf16[8,160,128]{2,1,0:T(8,128)(2,1)S(1)} %shard_map.37), channel_id=1, replica_groups={{0,32,64,96,128,160,192,224},{16,48,80,112,144,176,208,240},{1,33,65,97..., dimensions={0} | all-to-all | bytes 655360 | tf_op jit(solution)/shard_map/all_to_all | solution.py:208
  14.0 5.9 %collective-permute-start = (bf16[8,160,128]{2,1,0:T(8,128)(2,1)S(1)}, bf16[8,160,128]{2,1,0:T(8,128)(2,1)S(1)}, u32[]{:S(2)}, u32[]{:S(2)}) collective-permute-start(bf16[8,160,128]{2,1,0:T(8,128)(2,1)S(1)} %all_to_all.10.refs_2_), channel_id=1, source_target_pairs={{0,7},{1,0},{2,1},{3,2},{4,3},{5,4},{6,5},{7,6},{8,15},{9,8},{10,9... | collective-permute-start | bytes 983048 | tf_op jit(solution)/shard_map/ppermute | solution.py:57
  19.8 0.0 collective-permute-start.1
  19.8 0.0 collective-permute-start.2
  19.8 0.1 reshape.11.pattern_ref
  19.9 4.4 %shard_map.38.e_ref = bf16[2,5,2,160,1792]{4,3,2,1,0:T(8,128)(2,1)S(1)} custom-call(s32[1]{0:T(128)} %bitcast.1.here_ref, s32[1280]{0:T(1024)S(1)} %reshape.11.pattern_ref, bf16[5,2,160,2560]{3,2,1,0:T(8,128)(2,1)} %e_ref.1), custom_call_target="tpu_custom_call" | custom-call | bytes 8388608 | tf_op jit(solution)/shard_map/pallas_call | solution.py:124
  24.3 1.0 %collective-permute-done.refs_3_ = bf16[8,160,128]{2,1,0:T(8,128)(2,1)S(1)} collective-permute-done((bf16[8,160,128]{2,1,0:T(8,128)(2,1)S(1)}, bf16[8,160,128]{2,1,0:T(8,128)(2,1)S(1)}, u32[]{:S(2)}, u32[]{:S(2)}) %collective-permute-start) | collective-permute-done | bytes 327712 | tf_op jit(solution)/shard_map/ppermute | solution.py:57
  25.3 3.7 %collective-permute-start.6 = (bf16[8,160,128]{2,1,0:T(8,128)(2,1)S(1)}, bf16[8,160,128]{2,1,0:T(8,128)(2,1)S(1)}, u32[]{:S(2)}, u32[]{:S(2)}) collective-permute-start(bf16[8,160,128]{2,1,0:T(8,128)(2,1)S(1)} %collective-permute-done.refs_3_), channel_id=1, source_target_pairs={{0,7},{1,0},{2,1},{3,2},{4,3},{5,4},{6,5},{7,6},{8,15},{9,8},{10,9... | collective-permute-start | bytes 983048 | tf_op jit(solution)/shard_map/ppermute | solution.py:57
  29.0 0.6 collective-permute-start.4
  29.6 0.0 collective-permute-done.1.refs_1_
  29.7 4.0 %collective-permute-done.6.refs_0_ = bf16[8,160,128]{2,1,0:T(8,128)(2,1)S(1)} collective-permute-done((bf16[8,160,128]{2,1,0:T(8,128)(2,1)S(1)}, bf16[8,160,128]{2,1,0:T(8,128)(2,1)S(1)}, u32[]{:S(2)}, u32[]{:S(2)}) %collective-permute-start.6) | collective-permute-done | bytes 327712 | tf_op jit(solution)/shard_map/ppermute | solution.py:57
  33.6 3.7 %collective-permute-start.7 = (bf16[8,160,128]{2,1,0:T(8,128)(2,1)S(1)}, bf16[8,160,128]{2,1,0:T(8,128)(2,1)S(1)}, u32[]{:S(2)}, u32[]{:S(2)}) collective-permute-start(bf16[8,160,128]{2,1,0:T(8,128)(2,1)S(1)} %collective-permute-done.6.refs_0_), channel_id=1, source_target_pairs={{0,7},{1,0},{2,1},{3,2},{4,3},{5,4},{6,5},{7,6},{8,15},{9,8},{10,9... | collective-permute-start | bytes 983048 | tf_op jit(solution)/shard_map/ppermute | solution.py:57
  37.3 0.0 collective-permute-done.4.refs_3_
  37.3 1.4 %collective-permute-done.3.refs_0_ = bf16[8,160,128]{2,1,0:T(8,128)(2,1)S(1)} collective-permute-done((bf16[8,160,128]{2,1,0:T(8,128)(2,1)S(1)}, bf16[8,160,128]{2,1,0:T(8,128)(2,1)S(1)}, u32[]{:S(2)}, u32[]{:S(2)}) %collective-permute-start.3) | collective-permute-done | bytes 327712 | tf_op jit(solution)/shard_map/ppermute | solution.py:53
  38.7 1.8 %collective-permute-start.10 = (bf16[8,160,128]{2,1,0:T(8,128)(2,1)S(1)}, bf16[8,160,128]{2,1,0:T(8,128)(2,1)S(1)}, u32[]{:S(2)}, u32[]{:S(2)}) collective-permute-start(bf16[8,160,128]{2,1,0:T(8,128)(2,1)S(1)} %collective-permute-done.3.refs_0_), channel_id=1, source_target_pairs={{0,40},{1,41},{2,42},{3,43},{4,44},{5,45},{6,46},{7,47},{8,32},{9,... | collective-permute-start | bytes 983048 | tf_op jit(solution)/shard_map/ppermute | solution.py:61
  40.5 2.8 %shard_map.39.refs_4_ = f32[8,320,128]{2,1,0:T(8,128)S(1)} custom-call(s32[1]{0:T(128)} %bitcast.1.here_ref, bf16[2,5,2,160,1792]{4,3,2,1,0:T(8,128)(2,1)S(1)} %shard_map.38.e_ref, bf16[8,160,128]{2,1,0:T(8,128)(2,1)S(1)} %collective-permute-done.3.refs_0_, bf16[8,160,128]{2,1,0:T(8,128)(2,1)S(1)} %collective-permute-done.1.refs_1_, ...), custom_call_target="tpu_custom_call" | custom-call | flops 2516582400 | bytes 3145728 | tf_op jit(solution)/shard_map/pallas_call | solution.py:187
  43.3 0.0 collective-permute-done.7.refs_1_
  43.3 3.3 %collective-permute-start.12 = (bf16[8,160,128]{2,1,0:T(8,128)(2,1)S(1)}, bf16[8,160,128]{2,1,0:T(8,128)(2,1)S(1)}, u32[]{:S(2)}, u32[]{:S(2)}) collective-permute-start(bf16[8,160,128]{2,1,0:T(8,128)(2,1)S(1)} %collective-permute-done.7.refs_1_), channel_id=1, source_target_pairs={{0,7},{1,0},{2,1},{3,2},{4,3},{5,4},{6,5},{7,6},{8,15},{9,8},{10,9... | collective-permute-start | bytes 983048 | tf_op jit(solution)/shard_map/ppermute | solution.py:57
  46.6 0.3 collective-permute-start.5
  46.8 1.6 %collective-permute-done.14.refs_1_ = bf16[8,160,128]{2,1,0:T(8,128)(2,1)S(1)} collective-permute-done((bf16[8,160,128]{2,1,0:T(8,128)(2,1)S(1)}, bf16[8,160,128]{2,1,0:T(8,128)(2,1)S(1)}, u32[]{:S(2)}, u32[]{:S(2)}) %collective-permute-start.14) | collective-permute-done | bytes 327712 | tf_op jit(solution)/shard_map/ppermute | solution.py:53
  48.5 1.4 %collective-permute-start.8 = (bf16[8,160,128]{2,1,0:T(8,128)(2,1)S(1)}, bf16[8,160,128]{2,1,0:T(8,128)(2,1)S(1)}, u32[]{:S(2)}, u32[]{:S(2)}) collective-permute-start(bf16[8,160,128]{2,1,0:T(8,128)(2,1)S(1)} %collective-permute-done.7.refs_1_), channel_id=1, source_target_pairs={{0,40},{1,41},{2,42},{3,43},{4,44},{5,45},{6,46},{7,47},{8,32},{9,... | collective-permute-start | bytes 983048 | tf_op jit(solution)/shard_map/ppermute | solution.py:61
  49.9 2.8 %collective-permute-start.9 = (bf16[8,160,128]{2,1,0:T(8,128)(2,1)S(1)}, bf16[8,160,128]{2,1,0:T(8,128)(2,1)S(1)}, u32[]{:S(2)}, u32[]{:S(2)}) collective-permute-start(bf16[8,160,128]{2,1,0:T(8,128)(2,1)S(1)} %collective-permute-done.7.refs_1_), channel_id=1, source_target_pairs={{0,47},{1,40},{2,41},{3,42},{4,43},{5,44},{6,45},{7,46},{8,39},{9,... | collective-permute-start | bytes 983048 | tf_op jit(solution)/shard_map/ppermute | solution.py:65
  52.7 0.0 collective-permute-done.13.refs_3_
  52.7 2.8 %shard_map.40.refs_4_ = f32[8,320,128]{2,1,0:T(8,128)S(1)} custom-call(s32[1]{0:T(128)} %bitcast.1.here_ref, bf16[2,5,2,160,1792]{4,3,2,1,0:T(8,128)(2,1)S(1)} %shard_map.38.e_ref, bf16[8,160,128]{2,1,0:T(8,128)(2,1)S(1)} %collective-permute-done.10.refs_0_, bf16[8,160,128]{2,1,0:T(8,128)(2,1)S(1)} %collective-permute-done.14.refs_1_, ...), custom_call_target="tpu_custom_call" | custom-call | flops 2516582400 | bytes 3145728 | tf_op jit(solution)/shard_map/pallas_call | solution.py:187
  55.5 2.9 %shard_map.41.refs_4_ = f32[8,320,128]{2,1,0:T(8,128)S(1)} custom-call(s32[1]{0:T(128)} %bitcast.1.here_ref, bf16[2,5,2,160,1792]{4,3,2,1,0:T(8,128)(2,1)S(1)} %shard_map.38.e_ref, bf16[8,160,128]{2,1,0:T(8,128)(2,1)S(1)} %collective-permute-done.6.refs_0_, bf16[8,160,128]{2,1,0:T(8,128)(2,1)S(1)} %collective-permute-done.7.refs_1_, ...), custom_call_target="tpu_custom_call" | custom-call | flops 2516582400 | bytes 3145728 | tf_op jit(solution)/shard_map/pallas_call | solution.py:187
  58.4 1.0 %collective-permute-done.5.refs_0_ = bf16[8,160,128]{2,1,0:T(8,128)(2,1)S(1)} collective-permute-done((bf16[8,160,128]{2,1,0:T(8,128)(2,1)S(1)}, bf16[8,160,128]{2,1,0:T(8,128)(2,1)S(1)}, u32[]{:S(2)}, u32[]{:S(2)}) %collective-permute-start.5) | collective-permute-done | bytes 327712 | tf_op jit(solution)/shard_map/ppermute | solution.py:57
  59.5 3.5 %collective-permute-done.9.refs_2_ = bf16[8,160,128]{2,1,0:T(8,128)(2,1)S(1)} collective-permute-done((bf16[8,160,128]{2,1,0:T(8,128)(2,1)S(1)}, bf16[8,160,128]{2,1,0:T(8,128)(2,1)S(1)}, u32[]{:S(2)}, u32[]{:S(2)}) %collective-permute-start.9) | collective-permute-done | bytes 327712 | tf_op jit(solution)/shard_map/ppermute | solution.py:65
  63.0 3.0 %shard_map.42 = bf16[8,160,128]{2,1,0:T(8,128)(2,1)S(1)} custom-call(s32[1]{0:T(128)} %bitcast.1.here_ref, bf16[2,5,2,160,1792]{4,3,2,1,0:T(8,128)(2,1)S(1)} %shard_map.38.e_ref, bf16[8,160,128]{2,1,0:T(8,128)(2,1)S(1)} %collective-permute-done.5.refs_0_, bf16[8,160,128]{2,1,0:T(8,128)(2,1)S(1)} %collective-permute-done.8.refs_1_, ...), custom_call_target="tpu_custom_call" | custom-call | flops 2516582400 | bytes 3145728 | tf_op jit(solution)/shard_map/pallas_call | solution.py:187
  66.0 11.6 %all_to_all.11.pieces_ref = bf16[8,160,128]{2,1,0:T(8,128)(2,1)S(1)} all-to-all(bf16[8,160,128]{2,1,0:T(8,128)(2,1)S(1)} %shard_map.42), channel_id=1, replica_groups={{0,32,64,96,128,160,192,224},{16,48,80,112,144,176,208,240},{1,33,65,97..., dimensions={0} | all-to-all | bytes 655360 | tf_op jit(solution)/shard_map/all_to_all | solution.py:237
  77.5 0.9 %shard_map.43 = bf16[2,160,512]{2,1,0:T(8,128)(2,1)} custom-call(s32[1]{0:T(128)} %bitcast.flip_ref, bf16[8,160,128]{2,1,0:T(8,128)(2,1)S(1)} %all_to_all.11.pieces_ref), custom_call_target="tpu_custom_call" | custom-call | bytes 655360 | tf_op jit(solution)/shard_map/pallas_call | solution.py:86
  (12 shorter events, 0.0 us)
Async XLA Ops:
  0.0 1.0 %copy-start = (bf16[2,160,512]{2,1,0:T(8,128)(2,1)S(1)}, bf16[2,160,512]{2,1,0:T(8,128)(2,1)}, u32[]{:S(2)}) copy-start(bf16[2,160,512]{2,1,0:T(8,128)(2,1)} %x_ref.1) | copy-start | bytes 983044
  1.0 18.8 %copy-start.1 = (s32[5,16,16]{2,1,0:T(8,128)S(1)}, s32[5,16,16]{2,1,0:T(8,128)}, u32[]{:S(2)}) copy-start(s32[5,16,16]{2,1,0:T(8,128)} %param.5) | copy-start | bytes 15364
  14.0 11.4 %collective-permute-start = (bf16[8,160,128]{2,1,0:T(8,128)(2,1)S(1)}, bf16[8,160,128]{2,1,0:T(8,128)(2,1)S(1)}, u32[]{:S(2)}, u32[]{:S(2)}) collective-permute-start(bf16[8,160,128]{2,1,0:T(8,128)(2,1)S(1)} %all_to_all.10.refs_2_), channel_id=1, source_target_pairs={{0,7},{1,0},{2,1},{3,2},{4,3},{5,4},{6,5},{7,6},{8,15},{9,8},{10,9... | collective-permute-start | bytes 983048 | tf_op jit(solution)/shard_map/ppermute | solution.py:57
  19.8 9.8 %collective-permute-start.1 = (bf16[8,160,128]{2,1,0:T(8,128)(2,1)S(1)}, bf16[8,160,128]{2,1,0:T(8,128)(2,1)S(1)}, u32[]{:S(2)}, u32[]{:S(2)}) collective-permute-start(bf16[8,160,128]{2,1,0:T(8,128)(2,1)S(1)} %all_to_all.10.refs_2_), channel_id=1, source_target_pairs={{0,1},{1,2},{2,3},{3,4},{4,5},{5,6},{6,7},{7,0},{8,9},{9,10},{10,1... | collective-permute-start | bytes 983048 | tf_op jit(solution)/shard_map/ppermute | solution.py:53
  19.8 9.8 %collective-permute-start.2 = (bf16[8,160,128]{2,1,0:T(8,128)(2,1)S(1)}, bf16[8,160,128]{2,1,0:T(8,128)(2,1)S(1)}, u32[]{:S(2)}, u32[]{:S(2)}) collective-permute-start(bf16[8,160,128]{2,1,0:T(8,128)(2,1)S(1)} %all_to_all.10.refs_2_), channel_id=1, source_target_pairs={{0,40},{1,41},{2,42},{3,43},{4,44},{5,45},{6,46},{7,47},{8,32},{9,... | collective-permute-start | bytes 983048 | tf_op jit(solution)/shard_map/ppermute | solution.py:61
  25.3 8.3 %collective-permute-start.6 = (bf16[8,160,128]{2,1,0:T(8,128)(2,1)S(1)}, bf16[8,160,128]{2,1,0:T(8,128)(2,1)S(1)}, u32[]{:S(2)}, u32[]{:S(2)}) collective-permute-start(bf16[8,160,128]{2,1,0:T(8,128)(2,1)S(1)} %collective-permute-done.refs_3_), channel_id=1, source_target_pairs={{0,7},{1,0},{2,1},{3,2},{4,3},{5,4},{6,5},{7,6},{8,15},{9,8},{10,9... | collective-permute-start | bytes 983048 | tf_op jit(solution)/shard_map/ppermute | solution.py:57
  29.0 8.3 %collective-permute-start.4 = (bf16[8,160,128]{2,1,0:T(8,128)(2,1)S(1)}, bf16[8,160,128]{2,1,0:T(8,128)(2,1)S(1)}, u32[]{:S(2)}, u32[]{:S(2)}) collective-permute-start(bf16[8,160,128]{2,1,0:T(8,128)(2,1)S(1)} %collective-permute-done.refs_3_), channel_id=1, source_target_pairs={{0,40},{1,41},{2,42},{3,43},{4,44},{5,45},{6,46},{7,47},{8,32},{9,... | collective-permute-start | bytes 983048 | tf_op jit(solution)/shard_map/ppermute | solution.py:61
  29.6 9.0 %collective-permute-start.3 = (bf16[8,160,128]{2,1,0:T(8,128)(2,1)S(1)}, bf16[8,160,128]{2,1,0:T(8,128)(2,1)S(1)}, u32[]{:S(2)}, u32[]{:S(2)}) collective-permute-start(bf16[8,160,128]{2,1,0:T(8,128)(2,1)S(1)} %collective-permute-done.1.refs_1_), channel_id=1, source_target_pairs={{0,1},{1,2},{2,3},{3,4},{4,5},{5,6},{6,7},{7,0},{8,9},{9,10},{10,1... | collective-permute-start | bytes 983048 | tf_op jit(solution)/shard_map/ppermute | solution.py:53
  33.6 9.7 %collective-permute-start.7 = (bf16[8,160,128]{2,1,0:T(8,128)(2,1)S(1)}, bf16[8,160,128]{2,1,0:T(8,128)(2,1)S(1)}, u32[]{:S(2)}, u32[]{:S(2)}) collective-permute-start(bf16[8,160,128]{2,1,0:T(8,128)(2,1)S(1)} %collective-permute-done.6.refs_0_), channel_id=1, source_target_pairs={{0,7},{1,0},{2,1},{3,2},{4,3},{5,4},{6,5},{7,6},{8,15},{9,8},{10,9... | collective-permute-start | bytes 983048 | tf_op jit(solution)/shard_map/ppermute | solution.py:57
  37.3 11.2 %collective-permute-start.14 = (bf16[8,160,128]{2,1,0:T(8,128)(2,1)S(1)}, bf16[8,160,128]{2,1,0:T(8,128)(2,1)S(1)}, u32[]{:S(2)}, u32[]{:S(2)}) collective-permute-start(bf16[8,160,128]{2,1,0:T(8,128)(2,1)S(1)} %collective-permute-done.2.refs_2_), channel_id=1, source_target_pairs={{0,1},{1,2},{2,3},{3,4},{4,5},{5,6},{6,7},{7,0},{8,9},{9,10},{10,1... | collective-permute-start | bytes 983048 | tf_op jit(solution)/shard_map/ppermute | solution.py:53
  38.7 14.0 %collective-permute-start.13 = (bf16[8,160,128]{2,1,0:T(8,128)(2,1)S(1)}, bf16[8,160,128]{2,1,0:T(8,128)(2,1)S(1)}, u32[]{:S(2)}, u32[]{:S(2)}) collective-permute-start(bf16[8,160,128]{2,1,0:T(8,128)(2,1)S(1)} %collective-permute-done.3.refs_0_), channel_id=1, source_target_pairs={{0,1},{1,2},{2,3},{3,4},{4,5},{5,6},{6,7},{7,0},{8,9},{9,10},{10,1... | collective-permute-start | bytes 983048 | tf_op jit(solution)/shard_map/ppermute | solution.py:53
  38.7 11.2 %collective-permute-start.10 = (bf16[8,160,128]{2,1,0:T(8,128)(2,1)S(1)}, bf16[8,160,128]{2,1,0:T(8,128)(2,1)S(1)}, u32[]{:S(2)}, u32[]{:S(2)}) collective-permute-start(bf16[8,160,128]{2,1,0:T(8,128)(2,1)S(1)} %collective-permute-done.3.refs_0_), channel_id=1, source_target_pairs={{0,40},{1,41},{2,42},{3,43},{4,44},{5,45},{6,46},{7,47},{8,32},{9,... | collective-permute-start | bytes 983048 | tf_op jit(solution)/shard_map/ppermute | solution.py:61
  43.3 12.2 %collective-permute-start.12 = (bf16[8,160,128]{2,1,0:T(8,128)(2,1)S(1)}, bf16[8,160,128]{2,1,0:T(8,128)(2,1)S(1)}, u32[]{:S(2)}, u32[]{:S(2)}) collective-permute-start(bf16[8,160,128]{2,1,0:T(8,128)(2,1)S(1)} %collective-permute-done.7.refs_1_), channel_id=1, source_target_pairs={{0,7},{1,0},{2,1},{3,2},{4,3},{5,4},{6,5},{7,6},{8,15},{9,8},{10,9... | collective-permute-start | bytes 983048 | tf_op jit(solution)/shard_map/ppermute | solution.py:57
  46.6 12.9 %collective-permute-start.5 = (bf16[8,160,128]{2,1,0:T(8,128)(2,1)S(1)}, bf16[8,160,128]{2,1,0:T(8,128)(2,1)S(1)}, u32[]{:S(2)}, u32[]{:S(2)}) collective-permute-start(bf16[8,160,128]{2,1,0:T(8,128)(2,1)S(1)} %collective-permute-done.4.refs_3_), channel_id=1, source_target_pairs={{0,7},{1,0},{2,1},{3,2},{4,3},{5,4},{6,5},{7,6},{8,15},{9,8},{10,9... | collective-permute-start | bytes 983048 | tf_op jit(solution)/shard_map/ppermute | solution.py:57
  48.5 11.0 %collective-permute-start.8 = (bf16[8,160,128]{2,1,0:T(8,128)(2,1)S(1)}, bf16[8,160,128]{2,1,0:T(8,128)(2,1)S(1)}, u32[]{:S(2)}, u32[]{:S(2)}) collective-permute-start(bf16[8,160,128]{2,1,0:T(8,128)(2,1)S(1)} %collective-permute-done.7.refs_1_), channel_id=1, source_target_pairs={{0,40},{1,41},{2,42},{3,43},{4,44},{5,45},{6,46},{7,47},{8,32},{9,... | collective-permute-start | bytes 983048 | tf_op jit(solution)/shard_map/ppermute | solution.py:61
  49.9 13.1 %collective-permute-start.9 = (bf16[8,160,128]{2,1,0:T(8,128)(2,1)S(1)}, bf16[8,160,128]{2,1,0:T(8,128)(2,1)S(1)}, u32[]{:S(2)}, u32[]{:S(2)}) collective-permute-start(bf16[8,160,128]{2,1,0:T(8,128)(2,1)S(1)} %collective-permute-done.7.refs_1_), channel_id=1, source_target_pairs={{0,47},{1,40},{2,41},{3,42},{4,43},{5,44},{6,45},{7,46},{8,39},{9,... | collective-permute-start | bytes 983048 | tf_op jit(solution)/shard_map/ppermute | solution.py:65
  52.7 10.3 %collective-permute-start.11 = (bf16[8,160,128]{2,1,0:T(8,128)(2,1)S(1)}, bf16[8,160,128]{2,1,0:T(8,128)(2,1)S(1)}, u32[]{:S(2)}, u32[]{:S(2)}) collective-permute-start(bf16[8,160,128]{2,1,0:T(8,128)(2,1)S(1)} %collective-permute-done.10.refs_0_), channel_id=1, source_target_pairs={{0,1},{1,2},{2,3},{3,4},{4,5},{5,6},{6,7},{7,0},{8,9},{9,10},{10,1... | collective-permute-start | bytes 983048 | tf_op jit(solution)/shard_map/ppermute | solution.py:53

commit v3 on v2

--- a/solution.py
+++ b/solution.py
@@ -217,20 +217,19 @@
     own[1], own[-1], other[0] = down(own[0]), up(own[0]), across(own[0])
     ring = masked_ring(here, pattern, coupling)
     own[1], ring = tie((own[1], ring))
-    own[2], other[1] = down(own[1]), across(own[1])
-    own[-1], other[0] = tie((own[-1], other[0]))
-    own[-2] = up(own[-1])
+    own[2], own[-2] = down(own[1]), up(own[-1])
+    own[1], other[0] = tie((own[1], other[0]))
+    other[1] = across(own[1])
     own[3] = down(own[2])
     other[-2] = across(own[-2])
     own[-2], other[1] = tie((own[-2], other[1]))
     own[-3] = up(own[-2])
     other[-1] = up(other[0])
     other[2] = down(other[1])
-    acc = add(0, -2, None)
-    own[3], acc = tie((own[3], acc))
     own[4], other[3], other[4] = down(own[3]), across(own[3]), across_down(own[3])
     other[-3] = up(other[-2])
-    acc = add(1, -2, acc)
+    acc = add(1, -2, None)
+    acc = add(0, -2, acc)
     acc = add(0, 2, acc)
     result = add(1, 2, acc, last=True)
 

time: 78.6 us -> 78.7 us (level)
  waiting for transfers between devices: 12.5 us -> 10.3 us
  starting transfers between devices: 23.4 us -> 25.1 us
    ppermute x1, waiting for transfers between devices: 3.51 us -> 0.01 us  [across_down(): return lax.ppermute(value, MODE, ACROSS_DOWN)]
    ppermute x5, starting transfers between devices: 16.8 us -> 20.2 us  [down(): return lax.ppermute(value, MODE, DOWN)]
    ppermute x5, waiting for transfers between devices: 6.03 us -> 9.11 us  [down(): return lax.ppermute(value, MODE, DOWN)]
    ppermute x5, waiting for transfers between devices: 2.98 us -> 0.11 us  [up(): return lax.ppermute(value, MODE, UP)]
    ppermute x5, starting transfers between devices: 0.01 us -> 1.94 us  [up(): return lax.ppermute(value, MODE, UP)]
    ppermute x1, starting transfers between devices: 2.78 us -> 0.95 us  [across_down(): return lax.ppermute(value, MODE, ACROSS_DOWN)]
    ppermute x4, starting transfers between devices: 3.81 us -> 2.03 us  [across(): return lax.ppermute(value, MODE, ACROSS)]
    ppermute x4, waiting for transfers between devices: 0.01 us -> 1.05 us  [across(): return lax.ppermute(value, MODE, ACROSS)]
  transfers between devices with their start and end apart: 15 -> 15, of which waited for: 6 -> 5; matrix products, arithmetic and copies ran while one was open for 0% -> 0% of each run, Pallas kernels for 16% -> 16%
where the time goes in v3:
time: 78.7 us; the launch traced here: 78.5 us
  starting transfers between devices  25.1 us (32%)
  blocking collectives  25 us (32%)
  Pallas kernels  17 us (22%)
  waiting for transfers between devices  10.3 us (13%)
  local copies, waits for them, and re-layouts  1.05 us (1%)
    ppermute x5, starting transfers between devices, down(): return lax.ppermute(value, MODE, DOWN)  20.2 us
    all_to_all x1, blocking collectives, per_device(): lax.all_to_all(pieces, 'mode', 0, 0, axis_index_groups=GROUPS, tiled=True)  12.8 us
    all_to_all x1, blocking collectives, per_device(): lax.all_to_all(result, 'mode', 0, 0, axis_index_groups=GROUPS, tiled=True)  12.2 us
    pallas_call x4, Pallas kernels, run_product(): pl.pallas_call(functools.partial(run_kernel, far, start, first, last), ou...  11.5 us
    ppermute x5, waiting for transfers between devices, down(): return lax.ppermute(value, MODE, DOWN)  9.11 us
    pallas_call x1, Pallas kernels, masked_ring(): pl.pallas_call(mask_kernel, out_shape=jax.ShapeDtypeStruct((2, NOFF, 2, R...  4.39 us
    ppermute x4, starting transfers between devices, across(): return lax.ppermute(value, MODE, ACROSS)  2.03 us
    ppermute x5, starting transfers between devices, up(): return lax.ppermute(value, MODE, UP)  1.94 us
  transfers between devices with their start and end apart: 15, of which 5 were waited for; matrix products, arithmetic and copies ran while one was open for 0% of the time, Pallas kernels for 16%

profile of v3, /device:TPU:16, one launch (start us, length us, event | category | flops | bytes accessed | tf_op | source)
XLA Modules:
  0.0 78.5 jit_solution(8318597073573651387)
XLA Ops:
  0.0 1.0 %copy-done = bf16[2,160,512]{2,1,0:T(8,128)(2,1)S(1)} copy-done((bf16[2,160,512]{2,1,0:T(8,128)(2,1)S(1)}, bf16[2,160,512]{2,1,0:T(8,128)(2,1)}, u32[]{:S(2)}) %copy-start) | copy-done | bytes 327704
  1.0 0.1 shard_map.37
  1.1 12.8 %all_to_all.10.refs_2_ = bf16[8,160,128]{2,1,0:T(8,128)(2,1)S(1)} all-to-all(bf16[8,160,128]{2,1,0:T(8,128)(2,1)S(1)} %shard_map.37), channel_id=1, replica_groups={{0,32,64,96,128,160,192,224},{16,48,80,112,144,176,208,240},{1,33,65,97..., dimensions={0} | all-to-all | bytes 655360 | tf_op jit(solution)/shard_map/all_to_all | solution.py:208
  14.0 5.9 %collective-permute-start = (bf16[8,160,128]{2,1,0:T(8,128)(2,1)S(1)}, bf16[8,160,128]{2,1,0:T(8,128)(2,1)S(1)}, u32[]{:S(2)}, u32[]{:S(2)}) collective-permute-start(bf16[8,160,128]{2,1,0:T(8,128)(2,1)S(1)} %all_to_all.10.refs_2_), channel_id=1, source_target_pairs={{0,7},{1,0},{2,1},{3,2},{4,3},{5,4},{6,5},{7,6},{8,15},{9,8},{10,9... | collective-permute-start | bytes 983048 | tf_op jit(solution)/shard_map/ppermute | solution.py:57
  19.8 0.0 collective-permute-start.1
  19.8 0.0 collective-permute-start.3
  19.8 0.1 reshape.11.pattern_ref
  19.9 4.4 %shard_map.38.e_ref = bf16[2,5,2,160,1792]{4,3,2,1,0:T(8,128)(2,1)S(1)} custom-call(s32[1]{0:T(128)} %bitcast.1.here_ref, s32[1280]{0:T(1024)S(1)} %reshape.11.pattern_ref, bf16[5,2,160,2560]{3,2,1,0:T(8,128)(2,1)} %e_ref.1), custom_call_target="tpu_custom_call" | custom-call | bytes 8388608 | tf_op jit(solution)/shard_map/pallas_call | solution.py:124
  24.3 1.0 %collective-permute-done.refs_3_ = bf16[8,160,128]{2,1,0:T(8,128)(2,1)S(1)} collective-permute-done((bf16[8,160,128]{2,1,0:T(8,128)(2,1)S(1)}, bf16[8,160,128]{2,1,0:T(8,128)(2,1)S(1)}, u32[]{:S(2)}, u32[]{:S(2)}) %collective-permute-start) | collective-permute-done | bytes 327712 | tf_op jit(solution)/shard_map/ppermute | solution.py:57
  25.3 3.7 %collective-permute-start.6 = (bf16[8,160,128]{2,1,0:T(8,128)(2,1)S(1)}, bf16[8,160,128]{2,1,0:T(8,128)(2,1)S(1)}, u32[]{:S(2)}, u32[]{:S(2)}) collective-permute-start(bf16[8,160,128]{2,1,0:T(8,128)(2,1)S(1)} %collective-permute-done.refs_3_), channel_id=1, source_target_pairs={{0,7},{1,0},{2,1},{3,2},{4,3},{5,4},{6,5},{7,6},{8,15},{9,8},{10,9... | collective-permute-start | bytes 983048 | tf_op jit(solution)/shard_map/ppermute | solution.py:57
  29.0 0.0 collective-permute-done.1.refs_1_
  29.0 0.0 collective-permute-start.2
  29.0 0.0 collective-permute-done.3.refs_2_
  29.0 0.7 collective-permute-start.4
  29.7 3.9 %collective-permute-done.6.refs_0_ = bf16[8,160,128]{2,1,0:T(8,128)(2,1)S(1)} collective-permute-done((bf16[8,160,128]{2,1,0:T(8,128)(2,1)S(1)}, bf16[8,160,128]{2,1,0:T(8,128)(2,1)S(1)}, u32[]{:S(2)}, u32[]{:S(2)}) %collective-permute-start.6) | collective-permute-done | bytes 327712 | tf_op jit(solution)/shard_map/ppermute | solution.py:57
  33.6 3.7 %collective-permute-start.7 = (bf16[8,160,128]{2,1,0:T(8,128)(2,1)S(1)}, bf16[8,160,128]{2,1,0:T(8,128)(2,1)S(1)}, u32[]{:S(2)}, u32[]{:S(2)}) collective-permute-start(bf16[8,160,128]{2,1,0:T(8,128)(2,1)S(1)} %collective-permute-done.6.refs_0_), channel_id=1, source_target_pairs={{0,7},{1,0},{2,1},{3,2},{4,3},{5,4},{6,5},{7,6},{8,15},{9,8},{10,9... | collective-permute-start | bytes 983048 | tf_op jit(solution)/shard_map/ppermute | solution.py:57
  37.3 0.0 collective-permute-start.14
  37.3 0.1 collective-permute-done.2.refs_0_
  37.4 0.6 collective-permute-start.10
  38.0 3.2 %collective-permute-start.5 = (bf16[8,160,128]{2,1,0:T(8,128)(2,1)S(1)}, bf16[8,160,128]{2,1,0:T(8,128)(2,1)S(1)}, u32[]{:S(2)}, u32[]{:S(2)}) collective-permute-start(bf16[8,160,128]{2,1,0:T(8,128)(2,1)S(1)} %collective-permute-done.4.refs_3_), channel_id=1, source_target_pairs={{0,7},{1,0},{2,1},{3,2},{4,3},{5,4},{6,5},{7,6},{8,15},{9,8},{10,9... | collective-permute-start | bytes 983048 | tf_op jit(solution)/shard_map/ppermute | solution.py:57
  41.3 4.2 %collective-permute-done.7.refs_1_ = bf16[8,160,128]{2,1,0:T(8,128)(2,1)S(1)} collective-permute-done((bf16[8,160,128]{2,1,0:T(8,128)(2,1)S(1)}, bf16[8,160,128]{2,1,0:T(8,128)(2,1)S(1)}, u32[]{:S(2)}, u32[]{:S(2)}) %collective-permute-start.7) | collective-permute-done | bytes 327712 | tf_op jit(solution)/shard_map/ppermute | solution.py:57
  45.5 3.7 %collective-permute-start.12 = (bf16[8,160,128]{2,1,0:T(8,128)(2,1)S(1)}, bf16[8,160,128]{2,1,0:T(8,128)(2,1)S(1)}, u32[]{:S(2)}, u32[]{:S(2)}) collective-permute-start(bf16[8,160,128]{2,1,0:T(8,128)(2,1)S(1)} %collective-permute-done.7.refs_1_), channel_id=1, source_target_pairs={{0,7},{1,0},{2,1},{3,2},{4,3},{5,4},{6,5},{7,6},{8,15},{9,8},{10,9... | collective-permute-start | bytes 983048 | tf_op jit(solution)/shard_map/ppermute | solution.py:57
  49.2 0.7 collective-permute-start.8
  49.9 1.0 %collective-permute-start.9 = (bf16[8,160,128]{2,1,0:T(8,128)(2,1)S(1)}, bf16[8,160,128]{2,1,0:T(8,128)(2,1)S(1)}, u32[]{:S(2)}, u32[]{:S(2)}) collective-permute-start(bf16[8,160,128]{2,1,0:T(8,128)(2,1)S(1)} %collective-permute-done.7.refs_1_), channel_id=1, source_target_pairs={{0,47},{1,40},{2,41},{3,42},{4,43},{5,44},{6,45},{7,46},{8,39},{9,... | collective-permute-start | bytes 983048 | tf_op jit(solution)/shard_map/ppermute | solution.py:65
  50.8 2.8 %shard_map.39.refs_4_ = f32[8,320,128]{2,1,0:T(8,128)S(1)} custom-call(s32[1]{0:T(128)} %bitcast.1.here_ref, bf16[2,5,2,160,1792]{4,3,2,1,0:T(8,128)(2,1)S(1)} %shard_map.38.e_ref, bf16[8,160,128]{2,1,0:T(8,128)(2,1)S(1)} %collective-permute-done.10.refs_0_, bf16[8,160,128]{2,1,0:T(8,128)(2,1)S(1)} %collective-permute-done.14.refs_1_, ...), custom_call_target="tpu_custom_call" | custom-call | flops 2516582400 | bytes 3145728 | tf_op jit(solution)/shard_map/pallas_call | solution.py:187
  53.7 1.9 %collective-permute-start.11 = (bf16[8,160,128]{2,1,0:T(8,128)(2,1)S(1)}, bf16[8,160,128]{2,1,0:T(8,128)(2,1)S(1)}, u32[]{:S(2)}, u32[]{:S(2)}) collective-permute-start(bf16[8,160,128]{2,1,0:T(8,128)(2,1)S(1)} %collective-permute-done.10.refs_0_), channel_id=1, source_target_pairs={{0,1},{1,2},{2,3},{3,4},{4,5},{5,6},{6,7},{7,0},{8,9},{9,10},{10,1... | collective-permute-start | bytes 983048 | tf_op jit(solution)/shard_map/ppermute | solution.py:53
  55.6 2.8 %shard_map.40.refs_4_ = f32[8,320,128]{2,1,0:T(8,128)S(1)} custom-call(s32[1]{0:T(128)} %bitcast.1.here_ref, bf16[2,5,2,160,1792]{4,3,2,1,0:T(8,128)(2,1)S(1)} %shard_map.38.e_ref, bf16[8,160,128]{2,1,0:T(8,128)(2,1)S(1)} %collective-permute-done.2.refs_0_, bf16[8,160,128]{2,1,0:T(8,128)(2,1)S(1)} %collective-permute-done.1.refs_1_, ...), custom_call_target="tpu_custom_call" | custom-call | flops 2516582400 | bytes 3145728 | tf_op jit(solution)/shard_map/pallas_call | solution.py:187
  58.4 2.9 %shard_map.41.refs_4_ = f32[8,320,128]{2,1,0:T(8,128)S(1)} custom-call(s32[1]{0:T(128)} %bitcast.1.here_ref, bf16[2,5,2,160,1792]{4,3,2,1,0:T(8,128)(2,1)S(1)} %shard_map.38.e_ref, bf16[8,160,128]{2,1,0:T(8,128)(2,1)S(1)} %collective-permute-done.6.refs_0_, bf16[8,160,128]{2,1,0:T(8,128)(2,1)S(1)} %collective-permute-done.7.refs_1_, ...), custom_call_target="tpu_custom_call" | custom-call | flops 2516582400 | bytes 3145728 | tf_op jit(solution)/shard_map/pallas_call | solution.py:187
  61.3 1.0 %collective-permute-done.8.refs_1_ = bf16[8,160,128]{2,1,0:T(8,128)(2,1)S(1)} collective-permute-done((bf16[8,160,128]{2,1,0:T(8,128)(2,1)S(1)}, bf16[8,160,128]{2,1,0:T(8,128)(2,1)S(1)}, u32[]{:S(2)}, u32[]{:S(2)}) %collective-permute-start.8) | collective-permute-done | bytes 327712 | tf_op jit(solution)/shard_map/ppermute | solution.py:61
  62.4 3.0 %shard_map.42 = bf16[8,160,128]{2,1,0:T(8,128)(2,1)S(1)} custom-call(s32[1]{0:T(128)} %bitcast.1.here_ref, bf16[2,5,2,160,1792]{4,3,2,1,0:T(8,128)(2,1)S(1)} %shard_map.38.e_ref, bf16[8,160,128]{2,1,0:T(8,128)(2,1)S(1)} %collective-permute-done.5.refs_0_, bf16[8,160,128]{2,1,0:T(8,128)(2,1)S(1)} %collective-permute-done.8.refs_1_, ...), custom_call_target="tpu_custom_call" | custom-call | flops 2516582400 | bytes 3145728 | tf_op jit(solution)/shard_map/pallas_call | solution.py:187
  65.4 12.2 %all_to_all.11.pieces_ref = bf16[8,160,128]{2,1,0:T(8,128)(2,1)S(1)} all-to-all(bf16[8,160,128]{2,1,0:T(8,128)(2,1)S(1)} %shard_map.42), channel_id=1, replica_groups={{0,32,64,96,128,160,192,224},{16,48,80,112,144,176,208,240},{1,33,65,97..., dimensions={0} | all-to-all | bytes 655360 | tf_op jit(solution)/shard_map/all_to_all | solution.py:236
  77.6 0.9 %shard_map.43 = bf16[2,160,512]{2,1,0:T(8,128)(2,1)} custom-call(s32[1]{0:T(128)} %bitcast.flip_ref, bf16[8,160,128]{2,1,0:T(8,128)(2,1)S(1)} %all_to_all.11.pieces_ref), custom_call_target="tpu_custom_call" | custom-call | bytes 655360 | tf_op jit(solution)/shard_map/pallas_call | solution.py:86
  (12 shorter events, 0.0 us)
Async XLA Ops:
  0.0 1.0 %copy-start = (bf16[2,160,512]{2,1,0:T(8,128)(2,1)S(1)}, bf16[2,160,512]{2,1,0:T(8,128)(2,1)}, u32[]{:S(2)}) copy-start(bf16[2,160,512]{2,1,0:T(8,128)(2,1)} %x_ref.1) | copy-start | bytes 983044
  1.0 18.8 %copy-start.1 = (s32[5,16,16]{2,1,0:T(8,128)S(1)}, s32[5,16,16]{2,1,0:T(8,128)}, u32[]{:S(2)}) copy-start(s32[5,16,16]{2,1,0:T(8,128)} %param.5) | copy-start | bytes 15364
  14.0 11.4 %collective-permute-start = (bf16[8,160,128]{2,1,0:T(8,128)(2,1)S(1)}, bf16[8,160,128]{2,1,0:T(8,128)(2,1)S(1)}, u32[]{:S(2)}, u32[]{:S(2)}) collective-permute-start(bf16[8,160,128]{2,1,0:T(8,128)(2,1)S(1)} %all_to_all.10.refs_2_), channel_id=1, source_target_pairs={{0,7},{1,0},{2,1},{3,2},{4,3},{5,4},{6,5},{7,6},{8,15},{9,8},{10,9... | collective-permute-start | bytes 983048 | tf_op jit(solution)/shard_map/ppermute | solution.py:57
  19.8 9.2 %collective-permute-start.1 = (bf16[8,160,128]{2,1,0:T(8,128)(2,1)S(1)}, bf16[8,160,128]{2,1,0:T(8,128)(2,1)S(1)}, u32[]{:S(2)}, u32[]{:S(2)}) collective-permute-start(bf16[8,160,128]{2,1,0:T(8,128)(2,1)S(1)} %all_to_all.10.refs_2_), channel_id=1, source_target_pairs={{0,1},{1,2},{2,3},{3,4},{4,5},{5,6},{6,7},{7,0},{8,9},{9,10},{10,1... | collective-permute-start | bytes 983048 | tf_op jit(solution)/shard_map/ppermute | solution.py:53
  19.8 9.2 %collective-permute-start.3 = (bf16[8,160,128]{2,1,0:T(8,128)(2,1)S(1)}, bf16[8,160,128]{2,1,0:T(8,128)(2,1)S(1)}, u32[]{:S(2)}, u32[]{:S(2)}) collective-permute-start(bf16[8,160,128]{2,1,0:T(8,128)(2,1)S(1)} %all_to_all.10.refs_2_), channel_id=1, source_target_pairs={{0,40},{1,41},{2,42},{3,43},{4,44},{5,45},{6,46},{7,47},{8,32},{9,... | collective-permute-start | bytes 983048 | tf_op jit(solution)/shard_map/ppermute | solution.py:61
  25.3 8.3 %collective-permute-start.6 = (bf16[8,160,128]{2,1,0:T(8,128)(2,1)S(1)}, bf16[8,160,128]{2,1,0:T(8,128)(2,1)S(1)}, u32[]{:S(2)}, u32[]{:S(2)}) collective-permute-start(bf16[8,160,128]{2,1,0:T(8,128)(2,1)S(1)} %collective-permute-done.refs_3_), channel_id=1, source_target_pairs={{0,7},{1,0},{2,1},{3,2},{4,3},{5,4},{6,5},{7,6},{8,15},{9,8},{10,9... | collective-permute-start | bytes 983048 | tf_op jit(solution)/shard_map/ppermute | solution.py:57
  29.0 8.4 %collective-permute-start.2 = (bf16[8,160,128]{2,1,0:T(8,128)(2,1)S(1)}, bf16[8,160,128]{2,1,0:T(8,128)(2,1)S(1)}, u32[]{:S(2)}, u32[]{:S(2)}) collective-permute-start(bf16[8,160,128]{2,1,0:T(8,128)(2,1)S(1)} %collective-permute-done.1.refs_1_), channel_id=1, source_target_pairs={{0,1},{1,2},{2,3},{3,4},{4,5},{5,6},{6,7},{7,0},{8,9},{9,10},{10,1... | collective-permute-start | bytes 983048 | tf_op jit(solution)/shard_map/ppermute | solution.py:53
  29.0 9.0 %collective-permute-start.4 = (bf16[8,160,128]{2,1,0:T(8,128)(2,1)S(1)}, bf16[8,160,128]{2,1,0:T(8,128)(2,1)S(1)}, u32[]{:S(2)}, u32[]{:S(2)}) collective-permute-start(bf16[8,160,128]{2,1,0:T(8,128)(2,1)S(1)} %collective-permute-done.refs_3_), channel_id=1, source_target_pairs={{0,40},{1,41},{2,42},{3,43},{4,44},{5,45},{6,46},{7,47},{8,32},{9,... | collective-permute-start | bytes 983048 | tf_op jit(solution)/shard_map/ppermute | solution.py:61
  33.6 11.9 %collective-permute-start.7 = (bf16[8,160,128]{2,1,0:T(8,128)(2,1)S(1)}, bf16[8,160,128]{2,1,0:T(8,128)(2,1)S(1)}, u32[]{:S(2)}, u32[]{:S(2)}) collective-permute-start(bf16[8,160,128]{2,1,0:T(8,128)(2,1)S(1)} %collective-permute-done.6.refs_0_), channel_id=1, source_target_pairs={{0,7},{1,0},{2,1},{3,2},{4,3},{5,4},{6,5},{7,6},{8,15},{9,8},{10,9... | collective-permute-start | bytes 983048 | tf_op jit(solution)/shard_map/ppermute | solution.py:57
  37.3 11.9 %collective-permute-start.14 = (bf16[8,160,128]{2,1,0:T(8,128)(2,1)S(1)}, bf16[8,160,128]{2,1,0:T(8,128)(2,1)S(1)}, u32[]{:S(2)}, u32[]{:S(2)}) collective-permute-start(bf16[8,160,128]{2,1,0:T(8,128)(2,1)S(1)} %collective-permute-done.3.refs_2_), channel_id=1, source_target_pairs={{0,1},{1,2},{2,3},{3,4},{4,5},{5,6},{6,7},{7,0},{8,9},{9,10},{10,1... | collective-permute-start | bytes 983048 | tf_op jit(solution)/shard_map/ppermute | solution.py:53
  37.4 12.5 %collective-permute-start.10 = (bf16[8,160,128]{2,1,0:T(8,128)(2,1)S(1)}, bf16[8,160,128]{2,1,0:T(8,128)(2,1)S(1)}, u32[]{:S(2)}, u32[]{:S(2)}) collective-permute-start(bf16[8,160,128]{2,1,0:T(8,128)(2,1)S(1)} %collective-permute-done.2.refs_0_), channel_id=1, source_target_pairs={{0,40},{1,41},{2,42},{3,43},{4,44},{5,45},{6,46},{7,47},{8,32},{9,... | collective-permute-start | bytes 983048 | tf_op jit(solution)/shard_map/ppermute | solution.py:61
  38.0 15.6 %collective-permute-start.13 = (bf16[8,160,128]{2,1,0:T(8,128)(2,1)S(1)}, bf16[8,160,128]{2,1,0:T(8,128)(2,1)S(1)}, u32[]{:S(2)}, u32[]{:S(2)}) collective-permute-start(bf16[8,160,128]{2,1,0:T(8,128)(2,1)S(1)} %collective-permute-done.2.refs_0_), channel_id=1, source_target_pairs={{0,1},{1,2},{2,3},{3,4},{4,5},{5,6},{6,7},{7,0},{8,9},{9,10},{10,1... | collective-permute-start | bytes 983048 | tf_op jit(solution)/shard_map/ppermute | solution.py:53
  38.0 23.3 %collective-permute-start.5 = (bf16[8,160,128]{2,1,0:T(8,128)(2,1)S(1)}, bf16[8,160,128]{2,1,0:T(8,128)(2,1)S(1)}, u32[]{:S(2)}, u32[]{:S(2)}) collective-permute-start(bf16[8,160,128]{2,1,0:T(8,128)(2,1)S(1)} %collective-permute-done.4.refs_3_), channel_id=1, source_target_pairs={{0,7},{1,0},{2,1},{3,2},{4,3},{5,4},{6,5},{7,6},{8,15},{9,8},{10,9... | collective-permute-start | bytes 983048 | tf_op jit(solution)/shard_map/ppermute | solution.py:57
  45.5 13.0 %collective-permute-start.12 = (bf16[8,160,128]{2,1,0:T(8,128)(2,1)S(1)}, bf16[8,160,128]{2,1,0:T(8,128)(2,1)S(1)}, u32[]{:S(2)}, u32[]{:S(2)}) collective-permute-start(bf16[8,160,128]{2,1,0:T(8,128)(2,1)S(1)} %collective-permute-done.7.refs_1_), channel_id=1, source_target_pairs={{0,7},{1,0},{2,1},{3,2},{4,3},{5,4},{6,5},{7,6},{8,15},{9,8},{10,9... | collective-permute-start | bytes 983048 | tf_op jit(solution)/shard_map/ppermute | solution.py:57
  49.2 13.2 %collective-permute-start.8 = (bf16[8,160,128]{2,1,0:T(8,128)(2,1)S(1)}, bf16[8,160,128]{2,1,0:T(8,128)(2,1)S(1)}, u32[]{:S(2)}, u32[]{:S(2)}) collective-permute-start(bf16[8,160,128]{2,1,0:T(8,128)(2,1)S(1)} %collective-permute-done.7.refs_1_), channel_id=1, source_target_pairs={{0,40},{1,41},{2,42},{3,43},{4,44},{5,45},{6,46},{7,47},{8,32},{9,... | collective-permute-start | bytes 983048 | tf_op jit(solution)/shard_map/ppermute | solution.py:61
  49.9 12.5 %collective-permute-start.9 = (bf16[8,160,128]{2,1,0:T(8,128)(2,1)S(1)}, bf16[8,160,128]{2,1,0:T(8,128)(2,1)S(1)}, u32[]{:S(2)}, u32[]{:S(2)}) collective-permute-start(bf16[8,160,128]{2,1,0:T(8,128)(2,1)S(1)} %collective-permute-done.7.refs_1_), channel_id=1, source_target_pairs={{0,47},{1,40},{2,41},{3,42},{4,43},{5,44},{6,45},{7,46},{8,39},{9,... | collective-permute-start | bytes 983048 | tf_op jit(solution)/shard_map/ppermute | solution.py:65
  53.7 8.7 %collective-permute-start.11 = (bf16[8,160,128]{2,1,0:T(8,128)(2,1)S(1)}, bf16[8,160,128]{2,1,0:T(8,128)(2,1)S(1)}, u32[]{:S(2)}, u32[]{:S(2)}) collective-permute-start(bf16[8,160,128]{2,1,0:T(8,128)(2,1)S(1)} %collective-permute-done.10.refs_0_), channel_id=1, source_target_pairs={{0,1},{1,2},{2,3},{3,4},{4,5},{5,6},{6,7},{7,0},{8,9},{9,10},{10,1... | collective-permute-start | bytes 983048 | tf_op jit(solution)/shard_map/ppermute | solution.py:53

commit v4 on v2

--- a/solution.py
+++ b/solution.py
@@ -14,6 +14,7 @@
 NOFF = 2 * HMAX + 1
 Q = 8
 HALF = 64
+PIECE = ROWS // 2
 TILE = 2 * HALF
 CORES = 2
 WALL_Z = 8
@@ -65,29 +66,50 @@
     return lax.ppermute(value, MODE, ACROSS_DOWN)
 
 
-def pack_kernel(flip_ref, x_ref, out_ref):
+def pack_kernel(flip_ref, x_ref, out_ref, held_ref, sems):
     flip = flip_ref[0]
-    for c in range(Q):
-        cols = slice(c * HALF, (c + 1) * HALF)
-        out_ref[c ^ flip] = jnp.concatenate([x_ref[0, :, cols], x_ref[1, :, cols]], axis=1)
-
-
-def unpack_kernel(flip_ref, pieces_ref, out_ref):
+    copies = [
+        [
+            pltpu.make_async_copy(
+                x_ref.at[part, pl.ds(at * PIECE, PIECE)], held_ref.at[part, pl.ds(at * PIECE, PIECE)], sems.at[part, at]
+            )
+            for part in range(2)
+        ]
+        for at in range(2)
+    ]
+    for pair in copies:
+        for copy in pair:
+            copy.start()
+    for at, pair in enumerate(copies):
+        for copy in pair:
+            copy.wait()
+        rows = slice(at * PIECE, (at + 1) * PIECE)
+        for c in range(Q):
+            cols = slice(c * HALF, (c + 1) * HALF)
+            out_ref[c ^ flip, rows, :] = jnp.concatenate([held_ref[0, rows, cols], held_ref[1, rows, cols]], axis=1)
+
+
+def unpack_kernel(flip_ref, pieces_ref, out_ref, held_ref, sems):
     flip = flip_ref[0]
-    for t in range(Q // 2):
-        a = pieces_ref[(2 * t) ^ flip]
-        b = pieces_ref[(2 * t + 1) ^ flip]
-        cols = slice(t * TILE, (t + 1) * TILE)
-        out_ref[0, :, cols] = jnp.concatenate([a[:, :HALF], b[:, :HALF]], axis=1)
-        out_ref[1, :, cols] = jnp.concatenate([a[:, HALF:], b[:, HALF:]], axis=1)
-
-
-def small_call(kernel, flip, value, shape):
+    copies = [pltpu.make_async_copy(held_ref.at[part], out_ref.at[part], sems.at[part]) for part in range(2)]
+    for part in range(2):
+        lanes = slice(part * HALF, (part + 1) * HALF)
+        for t in range(Q // 2):
+            a = pieces_ref[(2 * t) ^ flip]
+            b = pieces_ref[(2 * t + 1) ^ flip]
+            held_ref[part, :, t * TILE:(t + 1) * TILE] = jnp.concatenate([a[:, lanes], b[:, lanes]], axis=1)
+        copies[part].start()
+    for copy in copies:
+        copy.wait()
+
+
+def small_call(kernel, flip, value, shape, spaces, held, sems):
     return pl.pallas_call(
         kernel,
         out_shape=jax.ShapeDtypeStruct(shape, value.dtype),
-        in_specs=[pl.BlockSpec(memory_space=pltpu.SMEM), pl.BlockSpec(memory_space=pltpu.VMEM)],
-        out_specs=pl.BlockSpec(memory_space=pltpu.VMEM),
+        in_specs=[pl.BlockSpec(memory_space=pltpu.SMEM), pl.BlockSpec(memory_space=spaces[0])],
+        out_specs=pl.BlockSpec(memory_space=spaces[1]),
+        scratch_shapes=[pltpu.VMEM(held, value.dtype), pltpu.SemaphoreType.DMA(sems)],
         compiler_params=pltpu.CompilerParams(vmem_limit_bytes=VMEM_BYTES),
         cost_estimate=pl.CostEstimate(flops=0, bytes_accessed=4 * value.size, transcendentals=0),
     )(flip, value)
@@ -204,7 +226,9 @@
     pattern = pattern.reshape(-1)
     tie = lax.optimization_barrier
 
-    pieces = small_call(pack_kernel, flip, vectors, (Q, ROWS, TILE))
+    far_vectors = pltpu.with_memory_space_constraint(vectors, pltpu.HBM)
+    hbm, vmem = pltpu.HBM, pltpu.VMEM
+    pieces = small_call(pack_kernel, flip, far_vectors, (Q, ROWS, TILE), (hbm, vmem), vectors.shape, (2, 2))
     block = lax.all_to_all(pieces, "mode", 0, 0, axis_index_groups=GROUPS, tiled=True)
 
     own, other = {0: block}, {}
@@ -235,7 +259,7 @@
     result = add(1, 2, acc, last=True)
 
     back = lax.all_to_all(result, "mode", 0, 0, axis_index_groups=GROUPS, tiled=True)
-    return small_call(unpack_kernel, flip, back, vectors.shape)
+    return small_call(unpack_kernel, flip, back, vectors.shape, (vmem, hbm), vectors.shape, (2,))
 
 
 def solution(mesh):

time: 78.6 us -> 78.8 us (level)
  Pallas kernels: 17 us -> 18 us
  local copies, waits for them, and re-layouts: 1.05 us -> 0.08 us
    pallas_call x2, Pallas kernels: 1.03 us -> 2.04 us  [small_call(): pl.pallas_call(kernel, out_shape=jax.ShapeDtypeStruct(shape, value.dtype)...]
    unnamed x4 -> x2, local copies, waits for them, and re-layouts: 0.98 us -> 0.01 us
where the time goes in v4:
time: 78.8 us; the launch traced here: 78.6 us
  blocking collectives  24.4 us (31%)
  starting transfers between devices  23.4 us (30%)
  Pallas kernels  18 us (23%)
  waiting for transfers between devices  12.5 us (16%)
    ppermute x5, starting transfers between devices, down(): return lax.ppermute(value, MODE, DOWN)  16.8 us
    all_to_all x1, blocking collectives, per_device(): lax.all_to_all(pieces, 'mode', 0, 0, axis_index_groups=GROUPS, tiled=True)  12.8 us
    all_to_all x1, blocking collectives, per_device(): lax.all_to_all(result, 'mode', 0, 0, axis_index_groups=GROUPS, tiled=True)  11.6 us
    pallas_call x4, Pallas kernels, run_product(): pl.pallas_call(functools.partial(run_kernel, far, start, first, last), ou...  11.6 us
    ppermute x5, waiting for transfers between devices, down(): return lax.ppermute(value, MODE, DOWN)  6.03 us
    pallas_call x1, Pallas kernels, masked_ring(): pl.pallas_call(mask_kernel, out_shape=jax.ShapeDtypeStruct((2, NOFF, 2, R...  4.39 us
    ppermute x4, starting transfers between devices, across(): return lax.ppermute(value, MODE, ACROSS)  3.81 us
    ppermute x1, waiting for transfers between devices, across_down(): return lax.ppermute(value, MODE, ACROSS_DOWN)  3.51 us
  transfers between devices with their start and end apart: 15, of which 6 were waited for; matrix products, arithmetic and copies ran while one was open for 0% of the time, Pallas kernels for 16%

profile of v4, /device:TPU:16, one launch (start us, length us, event | category | flops | bytes accessed | tf_op | source)
XLA Modules:
  0.0 78.6 jit_solution(6311750555164920281)
XLA Ops:
  0.0 1.2 %shard_map.37 = bf16[8,160,128]{2,1,0:T(8,128)(2,1)S(1)} custom-call(s32[1]{0:T(128)} %bitcast.flip_ref, bf16[2,160,512]{2,1,0:T(8,128)(2,1)} %x_ref.1), custom_call_target="tpu_custom_call" | custom-call | bytes 655360 | tf_op jit(solution)/shard_map/pallas_call | solution.py:107
  1.2 12.8 %all_to_all.10.refs_2_ = bf16[8,160,128]{2,1,0:T(8,128)(2,1)S(1)} all-to-all(bf16[8,160,128]{2,1,0:T(8,128)(2,1)S(1)} %shard_map.37), channel_id=1, replica_groups={{0,32,64,96,128,160,192,224},{16,48,80,112,144,176,208,240},{1,33,65,97..., dimensions={0} | all-to-all | bytes 655360 | tf_op jit(solution)/shard_map/all_to_all | solution.py:232
  14.0 5.9 %collective-permute-start = (bf16[8,160,128]{2,1,0:T(8,128)(2,1)S(1)}, bf16[8,160,128]{2,1,0:T(8,128)(2,1)S(1)}, u32[]{:S(2)}, u32[]{:S(2)}) collective-permute-start(bf16[8,160,128]{2,1,0:T(8,128)(2,1)S(1)} %all_to_all.10.refs_2_), channel_id=1, source_target_pairs={{0,7},{1,0},{2,1},{3,2},{4,3},{5,4},{6,5},{7,6},{8,15},{9,8},{10,9... | collective-permute-start | bytes 983048 | tf_op jit(solution)/shard_map/ppermute | solution.py:58
  19.9 0.0 collective-permute-start.1
  19.9 0.0 collective-permute-start.2
  19.9 0.1 reshape.11.pattern_ref
  20.0 4.4 %shard_map.38.e_ref = bf16[2,5,2,160,1792]{4,3,2,1,0:T(8,128)(2,1)S(1)} custom-call(s32[1]{0:T(128)} %bitcast.1.here_ref, s32[1280]{0:T(1024)S(1)} %reshape.11.pattern_ref, bf16[5,2,160,2560]{3,2,1,0:T(8,128)(2,1)} %e_ref.1), custom_call_target="tpu_custom_call" | custom-call | bytes 8388608 | tf_op jit(solution)/shard_map/pallas_call | solution.py:146
  24.4 1.0 %collective-permute-done.refs_3_ = bf16[8,160,128]{2,1,0:T(8,128)(2,1)S(1)} collective-permute-done((bf16[8,160,128]{2,1,0:T(8,128)(2,1)S(1)}, bf16[8,160,128]{2,1,0:T(8,128)(2,1)S(1)}, u32[]{:S(2)}, u32[]{:S(2)}) %collective-permute-start) | collective-permute-done | bytes 327712 | tf_op jit(solution)/shard_map/ppermute | solution.py:58
  25.4 3.7 %collective-permute-start.6 = (bf16[8,160,128]{2,1,0:T(8,128)(2,1)S(1)}, bf16[8,160,128]{2,1,0:T(8,128)(2,1)S(1)}, u32[]{:S(2)}, u32[]{:S(2)}) collective-permute-start(bf16[8,160,128]{2,1,0:T(8,128)(2,1)S(1)} %collective-permute-done.refs_3_), channel_id=1, source_target_pairs={{0,7},{1,0},{2,1},{3,2},{4,3},{5,4},{6,5},{7,6},{8,15},{9,8},{10,9... | collective-permute-start | bytes 983048 | tf_op jit(solution)/shard_map/ppermute | solution.py:58
  29.1 0.6 collective-permute-start.4
  29.7 0.0 collective-permute-done.1.refs_1_
  29.7 0.0 collective-permute-done.2.refs_2_
  29.7 4.0 %collective-permute-done.6.refs_0_ = bf16[8,160,128]{2,1,0:T(8,128)(2,1)S(1)} collective-permute-done((bf16[8,160,128]{2,1,0:T(8,128)(2,1)S(1)}, bf16[8,160,128]{2,1,0:T(8,128)(2,1)S(1)}, u32[]{:S(2)}, u32[]{:S(2)}) %collective-permute-start.6) | collective-permute-done | bytes 327712 | tf_op jit(solution)/shard_map/ppermute | solution.py:58
  33.7 3.7 %collective-permute-start.7 = (bf16[8,160,128]{2,1,0:T(8,128)(2,1)S(1)}, bf16[8,160,128]{2,1,0:T(8,128)(2,1)S(1)}, u32[]{:S(2)}, u32[]{:S(2)}) collective-permute-start(bf16[8,160,128]{2,1,0:T(8,128)(2,1)S(1)} %collective-permute-done.6.refs_0_), channel_id=1, source_target_pairs={{0,7},{1,0},{2,1},{3,2},{4,3},{5,4},{6,5},{7,6},{8,15},{9,8},{10,9... | collective-permute-start | bytes 983048 | tf_op jit(solution)/shard_map/ppermute | solution.py:58
  37.4 1.4 %collective-permute-done.3.refs_0_ = bf16[8,160,128]{2,1,0:T(8,128)(2,1)S(1)} collective-permute-done((bf16[8,160,128]{2,1,0:T(8,128)(2,1)S(1)}, bf16[8,160,128]{2,1,0:T(8,128)(2,1)S(1)}, u32[]{:S(2)}, u32[]{:S(2)}) %collective-permute-start.3) | collective-permute-done | bytes 327712 | tf_op jit(solution)/shard_map/ppermute | solution.py:54
  38.7 0.0 collective-permute-start.13
  38.7 1.8 %collective-permute-start.10 = (bf16[8,160,128]{2,1,0:T(8,128)(2,1)S(1)}, bf16[8,160,128]{2,1,0:T(8,128)(2,1)S(1)}, u32[]{:S(2)}, u32[]{:S(2)}) collective-permute-start(bf16[8,160,128]{2,1,0:T(8,128)(2,1)S(1)} %collective-permute-done.3.refs_0_), channel_id=1, source_target_pairs={{0,40},{1,41},{2,42},{3,43},{4,44},{5,45},{6,46},{7,47},{8,32},{9,... | collective-permute-start | bytes 983048 | tf_op jit(solution)/shard_map/ppermute | solution.py:62
  40.5 2.8 %shard_map.39.refs_4_ = f32[8,320,128]{2,1,0:T(8,128)S(1)} custom-call(s32[1]{0:T(128)} %bitcast.1.here_ref, bf16[2,5,2,160,1792]{4,3,2,1,0:T(8,128)(2,1)S(1)} %shard_map.38.e_ref, bf16[8,160,128]{2,1,0:T(8,128)(2,1)S(1)} %collective-permute-done.3.refs_0_, bf16[8,160,128]{2,1,0:T(8,128)(2,1)S(1)} %collective-permute-done.1.refs_1_, ...), custom_call_target="tpu_custom_call" | custom-call | flops 2516582400 | bytes 3145728 | tf_op jit(solution)/shard_map/pallas_call | solution.py:209
  43.4 3.3 %collective-permute-start.12 = (bf16[8,160,128]{2,1,0:T(8,128)(2,1)S(1)}, bf16[8,160,128]{2,1,0:T(8,128)(2,1)S(1)}, u32[]{:S(2)}, u32[]{:S(2)}) collective-permute-start(bf16[8,160,128]{2,1,0:T(8,128)(2,1)S(1)} %collective-permute-done.7.refs_1_), channel_id=1, source_target_pairs={{0,7},{1,0},{2,1},{3,2},{4,3},{5,4},{6,5},{7,6},{8,15},{9,8},{10,9... | collective-permute-start | bytes 983048 | tf_op jit(solution)/shard_map/ppermute | solution.py:58
  46.6 0.3 collective-permute-start.5
  46.9 1.6 %collective-permute-done.14.refs_1_ = bf16[8,160,128]{2,1,0:T(8,128)(2,1)S(1)} collective-permute-done((bf16[8,160,128]{2,1,0:T(8,128)(2,1)S(1)}, bf16[8,160,128]{2,1,0:T(8,128)(2,1)S(1)}, u32[]{:S(2)}, u32[]{:S(2)}) %collective-permute-start.14) | collective-permute-done | bytes 327712 | tf_op jit(solution)/shard_map/ppermute | solution.py:54
  48.5 1.4 %collective-permute-start.8 = (bf16[8,160,128]{2,1,0:T(8,128)(2,1)S(1)}, bf16[8,160,128]{2,1,0:T(8,128)(2,1)S(1)}, u32[]{:S(2)}, u32[]{:S(2)}) collective-permute-start(bf16[8,160,128]{2,1,0:T(8,128)(2,1)S(1)} %collective-permute-done.7.refs_1_), channel_id=1, source_target_pairs={{0,40},{1,41},{2,42},{3,43},{4,44},{5,45},{6,46},{7,47},{8,32},{9,... | collective-permute-start | bytes 983048 | tf_op jit(solution)/shard_map/ppermute | solution.py:62
  49.9 2.8 %collective-permute-start.9 = (bf16[8,160,128]{2,1,0:T(8,128)(2,1)S(1)}, bf16[8,160,128]{2,1,0:T(8,128)(2,1)S(1)}, u32[]{:S(2)}, u32[]{:S(2)}) collective-permute-start(bf16[8,160,128]{2,1,0:T(8,128)(2,1)S(1)} %collective-permute-done.7.refs_1_), channel_id=1, source_target_pairs={{0,47},{1,40},{2,41},{3,42},{4,43},{5,44},{6,45},{7,46},{8,39},{9,... | collective-permute-start | bytes 983048 | tf_op jit(solution)/shard_map/ppermute | solution.py:66
  52.7 2.8 %shard_map.40.refs_4_ = f32[8,320,128]{2,1,0:T(8,128)S(1)} custom-call(s32[1]{0:T(128)} %bitcast.1.here_ref, bf16[2,5,2,160,1792]{4,3,2,1,0:T(8,128)(2,1)S(1)} %shard_map.38.e_ref, bf16[8,160,128]{2,1,0:T(8,128)(2,1)S(1)} %collective-permute-done.10.refs_0_, bf16[8,160,128]{2,1,0:T(8,128)(2,1)S(1)} %collective-permute-done.14.refs_1_, ...), custom_call_target="tpu_custom_call" | custom-call | flops 2516582400 | bytes 3145728 | tf_op jit(solution)/shard_map/pallas_call | solution.py:209
  55.6 0.0 collective-permute-done.12.refs_2_
  55.6 2.9 %shard_map.41.refs_4_ = f32[8,320,128]{2,1,0:T(8,128)S(1)} custom-call(s32[1]{0:T(128)} %bitcast.1.here_ref, bf16[2,5,2,160,1792]{4,3,2,1,0:T(8,128)(2,1)S(1)} %shard_map.38.e_ref, bf16[8,160,128]{2,1,0:T(8,128)(2,1)S(1)} %collective-permute-done.6.refs_0_, bf16[8,160,128]{2,1,0:T(8,128)(2,1)S(1)} %collective-permute-done.7.refs_1_, ...), custom_call_target="tpu_custom_call" | custom-call | flops 2516582400 | bytes 3145728 | tf_op jit(solution)/shard_map/pallas_call | solution.py:209
  58.5 1.0 %collective-permute-done.5.refs_0_ = bf16[8,160,128]{2,1,0:T(8,128)(2,1)S(1)} collective-permute-done((bf16[8,160,128]{2,1,0:T(8,128)(2,1)S(1)}, bf16[8,160,128]{2,1,0:T(8,128)(2,1)S(1)}, u32[]{:S(2)}, u32[]{:S(2)}) %collective-permute-start.5) | collective-permute-done | bytes 327712 | tf_op jit(solution)/shard_map/ppermute | solution.py:58
  59.5 0.0 collective-permute-done.8.refs_1_
  59.5 3.5 %collective-permute-done.9.refs_2_ = bf16[8,160,128]{2,1,0:T(8,128)(2,1)S(1)} collective-permute-done((bf16[8,160,128]{2,1,0:T(8,128)(2,1)S(1)}, bf16[8,160,128]{2,1,0:T(8,128)(2,1)S(1)}, u32[]{:S(2)}, u32[]{:S(2)}) %collective-permute-start.9) | collective-permute-done | bytes 327712 | tf_op jit(solution)/shard_map/ppermute | solution.py:66
  63.0 3.0 %shard_map.42 = bf16[8,160,128]{2,1,0:T(8,128)(2,1)S(1)} custom-call(s32[1]{0:T(128)} %bitcast.1.here_ref, bf16[2,5,2,160,1792]{4,3,2,1,0:T(8,128)(2,1)S(1)} %shard_map.38.e_ref, bf16[8,160,128]{2,1,0:T(8,128)(2,1)S(1)} %collective-permute-done.5.refs_0_, bf16[8,160,128]{2,1,0:T(8,128)(2,1)S(1)} %collective-permute-done.8.refs_1_, ...), custom_call_target="tpu_custom_call" | custom-call | flops 2516582400 | bytes 3145728 | tf_op jit(solution)/shard_map/pallas_call | solution.py:209
  66.1 11.6 %all_to_all.11.pieces_ref = bf16[8,160,128]{2,1,0:T(8,128)(2,1)S(1)} all-to-all(bf16[8,160,128]{2,1,0:T(8,128)(2,1)S(1)} %shard_map.42), channel_id=1, replica_groups={{0,32,64,96,128,160,192,224},{16,48,80,112,144,176,208,240},{1,33,65,97..., dimensions={0} | all-to-all | bytes 655360 | tf_op jit(solution)/shard_map/all_to_all | solution.py:261
  77.6 0.8 %shard_map.43 = bf16[2,160,512]{2,1,0:T(8,128)(2,1)} custom-call(s32[1]{0:T(128)} %bitcast.flip_ref, bf16[8,160,128]{2,1,0:T(8,128)(2,1)S(1)} %all_to_all.11.pieces_ref), custom_call_target="tpu_custom_call" | custom-call | bytes 655360 | tf_op jit(solution)/shard_map/pallas_call | solution.py:107
  (10 shorter events, 0.0 us)
Async XLA Ops:
  0.0 19.9 %copy-start = (s32[5,16,16]{2,1,0:T(8,128)S(1)}, s32[5,16,16]{2,1,0:T(8,128)}, u32[]{:S(2)}) copy-start(s32[5,16,16]{2,1,0:T(8,128)} %param.5) | copy-start | bytes 15364
  14.0 11.4 %collective-permute-start = (bf16[8,160,128]{2,1,0:T(8,128)(2,1)S(1)}, bf16[8,160,128]{2,1,0:T(8,128)(2,1)S(1)}, u32[]{:S(2)}, u32[]{:S(2)}) collective-permute-start(bf16[8,160,128]{2,1,0:T(8,128)(2,1)S(1)} %all_to_all.10.refs_2_), channel_id=1, source_target_pairs={{0,7},{1,0},{2,1},{3,2},{4,3},{5,4},{6,5},{7,6},{8,15},{9,8},{10,9... | collective-permute-start | bytes 983048 | tf_op jit(solution)/shard_map/ppermute | solution.py:58
  19.9 9.8 %collective-permute-start.1 = (bf16[8,160,128]{2,1,0:T(8,128)(2,1)S(1)}, bf16[8,160,128]{2,1,0:T(8,128)(2,1)S(1)}, u32[]{:S(2)}, u32[]{:S(2)}) collective-permute-start(bf16[8,160,128]{2,1,0:T(8,128)(2,1)S(1)} %all_to_all.10.refs_2_), channel_id=1, source_target_pairs={{0,1},{1,2},{2,3},{3,4},{4,5},{5,6},{6,7},{7,0},{8,9},{9,10},{10,1... | collective-permute-start | bytes 983048 | tf_op jit(solution)/shard_map/ppermute | solution.py:54
  19.9 9.8 %collective-permute-start.2 = (bf16[8,160,128]{2,1,0:T(8,128)(2,1)S(1)}, bf16[8,160,128]{2,1,0:T(8,128)(2,1)S(1)}, u32[]{:S(2)}, u32[]{:S(2)}) collective-permute-start(bf16[8,160,128]{2,1,0:T(8,128)(2,1)S(1)} %all_to_all.10.refs_2_), channel_id=1, source_target_pairs={{0,40},{1,41},{2,42},{3,43},{4,44},{5,45},{6,46},{7,47},{8,32},{9,... | collective-permute-start | bytes 983048 | tf_op jit(solution)/shard_map/ppermute | solution.py:62
  25.4 8.3 %collective-permute-start.6 = (bf16[8,160,128]{2,1,0:T(8,128)(2,1)S(1)}, bf16[8,160,128]{2,1,0:T(8,128)(2,1)S(1)}, u32[]{:S(2)}, u32[]{:S(2)}) collective-permute-start(bf16[8,160,128]{2,1,0:T(8,128)(2,1)S(1)} %collective-permute-done.refs_3_), channel_id=1, source_target_pairs={{0,7},{1,0},{2,1},{3,2},{4,3},{5,4},{6,5},{7,6},{8,15},{9,8},{10,9... | collective-permute-start | bytes 983048 | tf_op jit(solution)/shard_map/ppermute | solution.py:58
  29.1 8.3 %collective-permute-start.4 = (bf16[8,160,128]{2,1,0:T(8,128)(2,1)S(1)}, bf16[8,160,128]{2,1,0:T(8,128)(2,1)S(1)}, u32[]{:S(2)}, u32[]{:S(2)}) collective-permute-start(bf16[8,160,128]{2,1,0:T(8,128)(2,1)S(1)} %collective-permute-done.refs_3_), channel_id=1, source_target_pairs={{0,40},{1,41},{2,42},{3,43},{4,44},{5,45},{6,46},{7,47},{8,32},{9,... | collective-permute-start | bytes 983048 | tf_op jit(solution)/shard_map/ppermute | solution.py:62
  29.7 9.0 %collective-permute-start.3 = (bf16[8,160,128]{2,1,0:T(8,128)(2,1)S(1)}, bf16[8,160,128]{2,1,0:T(8,128)(2,1)S(1)}, u32[]{:S(2)}, u32[]{:S(2)}) collective-permute-start(bf16[8,160,128]{2,1,0:T(8,128)(2,1)S(1)} %collective-permute-done.1.refs_1_), channel_id=1, source_target_pairs={{0,1},{1,2},{2,3},{3,4},{4,5},{5,6},{6,7},{7,0},{8,9},{9,10},{10,1... | collective-permute-start | bytes 983048 | tf_op jit(solution)/shard_map/ppermute | solution.py:54
  33.7 9.7 %collective-permute-start.7 = (bf16[8,160,128]{2,1,0:T(8,128)(2,1)S(1)}, bf16[8,160,128]{2,1,0:T(8,128)(2,1)S(1)}, u32[]{:S(2)}, u32[]{:S(2)}) collective-permute-start(bf16[8,160,128]{2,1,0:T(8,128)(2,1)S(1)} %collective-permute-done.6.refs_0_), channel_id=1, source_target_pairs={{0,7},{1,0},{2,1},{3,2},{4,3},{5,4},{6,5},{7,6},{8,15},{9,8},{10,9... | collective-permute-start | bytes 983048 | tf_op jit(solution)/shard_map/ppermute | solution.py:58
  37.4 11.2 %collective-permute-start.14 = (bf16[8,160,128]{2,1,0:T(8,128)(2,1)S(1)}, bf16[8,160,128]{2,1,0:T(8,128)(2,1)S(1)}, u32[]{:S(2)}, u32[]{:S(2)}) collective-permute-start(bf16[8,160,128]{2,1,0:T(8,128)(2,1)S(1)} %collective-permute-done.2.refs_2_), channel_id=1, source_target_pairs={{0,1},{1,2},{2,3},{3,4},{4,5},{5,6},{6,7},{7,0},{8,9},{9,10},{10,1... | collective-permute-start | bytes 983048 | tf_op jit(solution)/shard_map/ppermute | solution.py:54
  38.7 14.0 %collective-permute-start.13 = (bf16[8,160,128]{2,1,0:T(8,128)(2,1)S(1)}, bf16[8,160,128]{2,1,0:T(8,128)(2,1)S(1)}, u32[]{:S(2)}, u32[]{:S(2)}) collective-permute-start(bf16[8,160,128]{2,1,0:T(8,128)(2,1)S(1)} %collective-permute-done.3.refs_0_), channel_id=1, source_target_pairs={{0,1},{1,2},{2,3},{3,4},{4,5},{5,6},{6,7},{7,0},{8,9},{9,10},{10,1... | collective-permute-start | bytes 983048 | tf_op jit(solution)/shard_map/ppermute | solution.py:54
  38.7 11.2 %collective-permute-start.10 = (bf16[8,160,128]{2,1,0:T(8,128)(2,1)S(1)}, bf16[8,160,128]{2,1,0:T(8,128)(2,1)S(1)}, u32[]{:S(2)}, u32[]{:S(2)}) collective-permute-start(bf16[8,160,128]{2,1,0:T(8,128)(2,1)S(1)} %collective-permute-done.3.refs_0_), channel_id=1, source_target_pairs={{0,40},{1,41},{2,42},{3,43},{4,44},{5,45},{6,46},{7,47},{8,32},{9,... | collective-permute-start | bytes 983048 | tf_op jit(solution)/shard_map/ppermute | solution.py:62
  43.4 12.2 %collective-permute-start.12 = (bf16[8,160,128]{2,1,0:T(8,128)(2,1)S(1)}, bf16[8,160,128]{2,1,0:T(8,128)(2,1)S(1)}, u32[]{:S(2)}, u32[]{:S(2)}) collective-permute-start(bf16[8,160,128]{2,1,0:T(8,128)(2,1)S(1)} %collective-permute-done.7.refs_1_), channel_id=1, source_target_pairs={{0,7},{1,0},{2,1},{3,2},{4,3},{5,4},{6,5},{7,6},{8,15},{9,8},{10,9... | collective-permute-start | bytes 983048 | tf_op jit(solution)/shard_map/ppermute | solution.py:58
  46.6 12.9 %collective-permute-start.5 = (bf16[8,160,128]{2,1,0:T(8,128)(2,1)S(1)}, bf16[8,160,128]{2,1,0:T(8,128)(2,1)S(1)}, u32[]{:S(2)}, u32[]{:S(2)}) collective-permute-start(bf16[8,160,128]{2,1,0:T(8,128)(2,1)S(1)} %collective-permute-done.4.refs_3_), channel_id=1, source_target_pairs={{0,7},{1,0},{2,1},{3,2},{4,3},{5,4},{6,5},{7,6},{8,15},{9,8},{10,9... | collective-permute-start | bytes 983048 | tf_op jit(solution)/shard_map/ppermute | solution.py:58
  48.5 11.0 %collective-permute-start.8 = (bf16[8,160,128]{2,1,0:T(8,128)(2,1)S(1)}, bf16[8,160,128]{2,1,0:T(8,128)(2,1)S(1)}, u32[]{:S(2)}, u32[]{:S(2)}) collective-permute-start(bf16[8,160,128]{2,1,0:T(8,128)(2,1)S(1)} %collective-permute-done.7.refs_1_), channel_id=1, source_target_pairs={{0,40},{1,41},{2,42},{3,43},{4,44},{5,45},{6,46},{7,47},{8,32},{9,... | collective-permute-start | bytes 983048 | tf_op jit(solution)/shard_map/ppermute | solution.py:62
  49.9 13.1 %collective-permute-start.9 = (bf16[8,160,128]{2,1,0:T(8,128)(2,1)S(1)}, bf16[8,160,128]{2,1,0:T(8,128)(2,1)S(1)}, u32[]{:S(2)}, u32[]{:S(2)}) collective-permute-start(bf16[8,160,128]{2,1,0:T(8,128)(2,1)S(1)} %collective-permute-done.7.refs_1_), channel_id=1, source_target_pairs={{0,47},{1,40},{2,41},{3,42},{4,43},{5,44},{6,45},{7,46},{8,39},{9,... | collective-permute-start | bytes 983048 | tf_op jit(solution)/shard_map/ppermute | solution.py:66
  52.7 10.3 %collective-permute-start.11 = (bf16[8,160,128]{2,1,0:T(8,128)(2,1)S(1)}, bf16[8,160,128]{2,1,0:T(8,128)(2,1)S(1)}, u32[]{:S(2)}, u32[]{:S(2)}) collective-permute-start(bf16[8,160,128]{2,1,0:T(8,128)(2,1)S(1)} %collective-permute-done.10.refs_0_), channel_id=1, source_target_pairs={{0,1},{1,2},{2,3},{3,4},{4,5},{5,6},{6,7},{7,0},{8,9},{9,10},{10,1... | collective-permute-start | bytes 983048 | tf_op jit(solution)/shard_map/ppermute | solution.py:54
